TPU v7x, 256 devices: a whole 4x4x8 slice. The times are simulated.
256 devices in a mesh: grp: 8 (over x_lo, y), ctx: 32 (over z, x_hi, core).
Axes of the slice: x: 4 (x_hi: 2, x_lo: 2; x = x_hi * 2 + x_lo), y: 4, z: 8, core: 2. Of those that a mesh axis runs over, the one named last changes fastest.
Arguments:
- prompt_k: bfloat16 [512, 2048], P(('grp', 'ctx')), may hold values from -7 to 7
- prompt_v: bfloat16 [512, 2048], P(('grp', 'ctx')), may hold values from -6 to 6
- comp_q: bfloat16 [8, 32, 128, 2048], P('grp', 'ctx'), may hold values from -120 to 120
- comp_k: bfloat16 [8, 32, 128, 2048], P('grp', 'ctx'), may hold values from -6 to 6
- comp_v: bfloat16 [8, 32, 128, 2048], P('grp', 'ctx'), may hold values from -6 to 6
- grad_out: bfloat16 [8, 32, 64, 2048], P('grp', 'ctx'), may hold values from -24 to 24
- rewards: float32 [8, 32], P('grp', 'ctx'), may hold values from -4 to 4
- mask_pos: int32 [8, 32, 64], P('grp', 'ctx'), may hold values from 0 to 128, as said below
Outputs:
- grad_query: bfloat16 [8, 32, 64, 2048], P('grp', 'ctx')
- grad_comp_k: bfloat16 [8, 32, 128, 2048], P('grp', 'ctx')
- grad_comp_v: bfloat16 [8, 32, 128, 2048], P('grp', 'ctx')
- grad_prompt_k: bfloat16 [512, 2048], P(('grp', 'ctx'))
- grad_prompt_v: bfloat16 [512, 2048], P(('grp', 'ctx'))
Inputs may be any that keep to these rules, and one draw needn't show every extreme that they name: `mask_pos`: each completion lists its masked positions in increasing order, each once, then 128 in every unused slot; every completion has 16 or more masked positions, and in every group some completion has exactly 64.
All inputs are finite; a program needn't handle non-finite values.
Results may differ from a plain program's by a relative error of at most 0.015.
Values may be sent and summed in bfloat16 or wider, within the bound.
A program may use at most 128 MiB of HBM per device.

v0:
```python
import jax
import jax.numpy as jnp
from jax import lax
from jax.sharding import PartitionSpec as P

HEADS = 16
HEAD_DIM = 128


def output_products(form, left, right):
    return jnp.einsum(form, left, right, preferred_element_type=jnp.float32)


def attention_grads(query_rows, weighted, prompt_keys, prompt_values, own_keys, own_values):
    slot_count = query_rows.shape[0]
    features = query_rows.shape[1]
    logit_scale_factor = HEAD_DIM ** (-0.5)
    query_head_rows = query_rows.reshape(slot_count, HEADS, HEAD_DIM)
    gradient_heads = weighted.reshape(slot_count, HEADS, HEAD_DIM)
    context_key_heads = prompt_keys.reshape(-1, HEADS, HEAD_DIM)
    context_value_heads = prompt_values.reshape(-1, HEADS, HEAD_DIM)
    self_key_heads = own_keys.reshape(-1, HEADS, HEAD_DIM)
    self_value_heads = own_values.reshape(-1, HEADS, HEAD_DIM)
    context_scores = (
        output_products("eon,con->oec", query_head_rows, context_key_heads) * logit_scale_factor
    )
    self_scores = (
        output_products("skf,gkf->ksg", query_head_rows, self_key_heads) * logit_scale_factor
    )
    row_max = jnp.maximum(jnp.max(context_scores, axis=-1), jnp.max(self_scores, axis=-1))[
        ..., None
    ]
    exp_prompt = jnp.exp(context_scores - row_max)
    exp_own = jnp.exp(self_scores - row_max)
    denom = jnp.sum(exp_prompt, axis=-1, keepdims=True) + jnp.sum(exp_own, axis=-1, keepdims=True)
    prob_prompt = exp_prompt / denom
    prob_own = exp_own / denom
    rounded_context_probs = prob_prompt.astype(jnp.bfloat16)
    rounded_self_probs = prob_own.astype(jnp.bfloat16)
    attended_output = output_products(
        "uls,suo->luo", rounded_context_probs, context_value_heads
    ) + output_products("xwz,zxn->wxn", rounded_self_probs, self_value_heads)
    inner_sums = jnp.transpose(
        jnp.sum(gradient_heads.astype(jnp.float32) * attended_output, axis=-1)
    )[..., None]
    probability_grad_context = output_products("eon,con->oec", gradient_heads, context_value_heads)
    probability_grad_self = output_products("skf,gkf->ksg", gradient_heads, self_value_heads)
    score_grad_context = (prob_prompt * (probability_grad_context - inner_sums)).astype(
        jnp.bfloat16
    )
    score_grad_self = (prob_own * (probability_grad_self - inner_sums)).astype(jnp.bfloat16)
    gradient_query_rows = (
        output_products("uls,suo->luo", score_grad_context, context_key_heads)
        + output_products("xwz,zxn->wxn", score_grad_self, self_key_heads)
    ) * logit_scale_factor
    gradient_context_key = (
        output_products("uvt,vus->tus", score_grad_context, query_head_rows) * logit_scale_factor
    )
    gradient_context_value = output_products("uvt,vus->tus", rounded_context_probs, gradient_heads)
    gradient_self_key = (
        output_products("iou,oig->uig", score_grad_self, query_head_rows) * logit_scale_factor
    )
    gradient_self_value = output_products("iou,oig->uig", rounded_self_probs, gradient_heads)
    return (
        gradient_query_rows.reshape(slot_count, features),
        gradient_context_key.reshape(-1, features),
        gradient_context_value.reshape(-1, features),
        gradient_self_key.reshape(-1, features),
        gradient_self_value.reshape(-1, features),
    )


def shards(prompt_k, prompt_v, comp_q, comp_k, comp_v, grad_out, rewards, mask_pos):
    comp_len = comp_q.shape[2]
    slot_count = mask_pos.shape[2]
    positions = mask_pos[0, 0]
    is_masked = positions < comp_len
    masked_count = jnp.sum(is_masked.astype(jnp.float32))
    group_count, reward_total = lax.psum((masked_count, rewards[0, 0]), "ctx")
    members = lax.axis_size("ctx")
    advantage = rewards[0, 0] - reward_total / members
    token_weight = advantage * (slot_count * members) / group_count
    slot_rows = jnp.clip(positions, 0, comp_len - 1)
    query_rows = jnp.take(comp_q[0, 0], slot_rows, axis=0)
    weighted = (
        grad_out[0, 0].astype(jnp.float32) * jnp.where(is_masked, token_weight, 0.0)[:, None]
    ).astype(jnp.bfloat16)
    whole_keys, whole_values = (
        lax.all_gather(prompt_k, ("grp", "ctx"), axis=0, tiled=True),
        lax.all_gather(prompt_v, ("grp", "ctx"), axis=0, tiled=True),
    )
    (
        gradient_query_rows,
        gradient_context_key,
        gradient_context_value,
        gradient_self_key,
        gradient_self_value,
    ) = attention_grads(query_rows, weighted, whole_keys, whole_values, comp_k[0, 0], comp_v[0, 0])
    final_k, final_v = (
        lax.psum_scatter(gradient_context_key, ("grp", "ctx"), scatter_dimension=0, tiled=True),
        lax.psum_scatter(gradient_context_value, ("grp", "ctx"), scatter_dimension=0, tiled=True),
    )
    grad_query = gradient_query_rows.astype(jnp.bfloat16)[None, None]
    grad_comp_k = gradient_self_key.astype(jnp.bfloat16)[None, None]
    grad_comp_v = gradient_self_value.astype(jnp.bfloat16)[None, None]
    return (
        grad_query,
        grad_comp_k,
        grad_comp_v,
        final_k.astype(jnp.bfloat16),
        final_v.astype(jnp.bfloat16),
    )


def solution(mesh):
    in_specs = (
        P(("grp", "ctx"), None),
        P(("grp", "ctx"), None),
        P("grp", "ctx", None, None),
        P("grp", "ctx", None, None),
        P("grp", "ctx", None, None),
        P("grp", "ctx", None, None),
        P("grp", "ctx"),
        P("grp", "ctx", None),
    )
    out_specs = (
        P("grp", "ctx", None, None),
        P("grp", "ctx", None, None),
        P("grp", "ctx", None, None),
        P(("grp", "ctx"), None),
        P(("grp", "ctx"), None),
    )
    return jax.shard_map(shards, mesh=mesh, in_specs=in_specs, out_specs=out_specs, check_vma=False)
```

profile of v0, /device:TPU:1, one launch (start us, length us, event | category | flops | bytes accessed | tf_op | source)
XLA Modules:
  0.0 1012.2 jit_solution(2532234026017696804)
XLA Ops:
  8.7 1.3 fusion.52
  10.0 69.6 %all-reduce.3 = (f32[]{:T(128)}, f32[]{:T(128)}) all-reduce(f32[]{:T(128)} %bitcast.5, f32[]{:T(128)} %fusion.52), channel_id=1, replica_groups=mesh['grp'=8,'ctx'=32] {'ctx'}, use_global_device_ids=true, to_apply=%region_4.5 | all-reduce | flops 2 | bytes 16 | tf_op jit(solution)/shard_map/psum | solution.py:79
  80.2 1.0 convert_bitcast_fusion
  81.3 0.9 copy.55
  85.4 1.3 fusion.59
  86.7 333.8 %all-gather.5.cloned.1.call-done = bf16[256,2,2048]{2,1,0:T(2,128)(2,1)} async-done(((bf16[1,2,2048]{2,1,0:T(2,128)(2,1)}), bf16[256,2,2048]{2,1,0:T(2,128)(2,1)}) %all-gather.5.cloned.1.call-update) | async-done | bytes 2097168 | tf_op jit(solution)/shard_map/all_gather | solution.py:89
  420.5 3.2 reshape.128
  423.7 1.2 multiply_reduce_fusion
  425.3 0.9 copy-done.1
  426.8 1.3 fusion.46
  428.1 399.5 %all-gather.7.cloned.1.call-done = bf16[256,2,2048]{2,1,0:T(2,128)(2,1)} async-done(((bf16[1,2,2048]{2,1,0:T(2,128)(2,1)}), bf16[256,2,2048]{2,1,0:T(2,128)(2,1)}) %all-gather.7.cloned.1.call-update) | async-done | bytes 2097168 | tf_op jit(solution)/shard_map/all_gather | solution.py:90
  827.6 4.4 reshape.129
  832.0 4.1 fusion.33
  836.7 1.0 copy-done.2
  837.7 1.7 multiply_convert_fusion
  840.1 1.4 convolution_convert_fusion
  841.5 2.8 fusion.40
  844.3 2.8 convolution_multiply_fusion
  849.0 1.0 copy.50
  850.0 1.0 copy.51
  851.0 5.4 copy.48
  856.4 5.4 copy.49
  861.8 142.2 %all-reduce.5 = (bf16[512,2048]{1,0:T(8,128)(2,1)S(1)}, bf16[512,2048]{1,0:T(8,128)(2,1)}) all-reduce(f32[512,2048]{1,0:T(8,128)} %copy.48, f32[512,2048]{1,0:T(8,128)} %copy.49), channel_id=2, replica_groups=mesh['grp'=8,'ctx'=32] {'grp','ctx'}, use_global_device_ids=true, to_apply=%region_8.9.clone | all-reduce | flops 2097152 | bytes 12582912
  1004.0 1.4 dynamic-slice_convert_fusion
  (46 shorter events, 7.5 us)
Async XLA Ops:
  7.2 76.5 %copy-start = (bf16[1,1,128,2048]{3,2,1,0:T(8,128)(2,1)S(1)}, bf16[1,1,128,2048]{3,2,1,0:T(8,128)(2,1)}, u32[]{:S(2)}) copy-start(bf16[1,1,128,2048]{3,2,1,0:T(8,128)(2,1)} %param.10) | copy-start | bytes 1572868
  7.2 76.5 %copy-start.12 = (s32[1,1,64]{2,1,0:T(1,128)S(1)}, s32[1,1,64]{2,1,0:T(1,128)}, u32[]{:S(2)}) copy-start(s32[1,1,64]{2,1,0:T(1,128)} %param.15) | copy-start | bytes 772
  7.2 74.1 %copy-start.4 = (bf16[1,1,128,2048]{3,2,1,0:T(8,128)(2,1)S(1)}, bf16[1,1,128,2048]{3,2,1,0:T(8,128)(2,1)}, u32[]{:S(2)}) copy-start(bf16[1,1,128,2048]{3,2,1,0:T(8,128)(2,1)} %param.12) | copy-start | bytes 1572868
  7.2 75.0 %copy-start.5 = (bf16[1,1,128,2048]{3,2,1,0:T(8,128)(2,1)S(1)}, bf16[1,1,128,2048]{3,2,1,0:T(8,128)(2,1)}, u32[]{:S(2)}) copy-start(bf16[1,1,128,2048]{3,2,1,0:T(8,128)(2,1)} %param.11) | copy-start | bytes 1572868
  7.2 413.3 %all-gather.5.cloned.1.call-start = ((), (), s32[]{:S(2)}) async-start(), calls=%async_computation | async-start | bytes 2105344 | tf_op jit(solution)/shard_map/all_gather | solution.py:89
  7.9 819.7 %all-gather.7.cloned.1.call-start = ((), (), s32[]{:S(2)}) async-start(), calls=%async_computation.1 | async-start | bytes 2105344 | tf_op jit(solution)/shard_map/all_gather | solution.py:90
  423.6 1.2 copy-start.8
  424.9 1.4 copy-start.1
  424.9 2.0 copy-start.6
  832.0 4.1 copy-start.7
  832.0 4.1 copy-start.9
  832.0 4.1 copy-start.11
  832.0 4.7 copy-start.3
  836.1 1.6 copy-start.2
  848.0 2.0 copy-start.10
Sparse Core Ops, SparseCore 0:
  9.9 410.5 all-gather.4
  422.4 405.2 all-gather.6
where the time goes:
time: 1010 us
  waiting for transfers between devices  735 us (73%)
  blocking collectives  212 us (21%)
  local copies, waits for them, and re-layouts  26.5 us (3%)
  matrix products  18.7 us (2%)
  between operations  16.3 us (2%)
    all_gather x1, waiting for transfers between devices, shards(): lax.all_gather(prompt_v, ('grp', 'ctx'), axis=0, tiled=True)  400 us
    all_gather x1, waiting for transfers between devices, shards(): lax.all_gather(prompt_k, ('grp', 'ctx'), axis=0, tiled=True)  334 us
    unnamed x1, blocking collectives  142 us
    psum x1, blocking collectives, shards(): group_count, reward_total = lax.psum((masked_count, rewards[0, 0]), 'ctx')  69.6 us
  transfers between devices with their start and end apart: 2, of which 2 were waited for; matrix products, arithmetic and copies ran while one was open for 1% of the time, Pallas kernels for 0%

commit v1 on v0

v1 whole, which is shorter than its diff:
```python
import jax
import jax.numpy as jnp
from jax import lax
from jax.experimental import pallas as pl
from jax.experimental.pallas import tpu as pltpu
from jax.sharding import PartitionSpec as P

HEADS = 16
DIM = 128
SLOTS = 64
ROWS = 128
WIDTH = 2048
PROMPT = 512
F32 = jnp.float32
BF16 = jnp.bfloat16
SCALE = DIM ** -0.5
SCALE2 = SCALE * 1.4426950408889634
MESH = pl.DeviceIdType.MESH

KV, QG, ZKV, ZSUM, YKV, OWN, FIN, DQ, RS1, RS2, RS3, KINDS = range(12)


def dot_nt(a, b):
    return lax.dot_general(a, b, (((1,), (1,)), ((), ())), preferred_element_type=F32)


def dot_nn(a, b):
    return lax.dot_general(a, b, (((1,), (0,)), ((), ())), preferred_element_type=F32)


def dot_tn(a, b):
    return lax.dot_general(a, b, (((0,), (0,)), ((), ())), preferred_element_type=F32)


def kernel(
    pk_hbm, pv_hbm, rw_hbm, mp_hbm, cq_hbm, ck_hbm, cv_hbm, go_hbm,
    dq_hbm, dk_hbm, dv_hbm, gk_hbm, gv_hbm,
    pk, pv, rw, mp, cq, ck, cv, go, xb, xbr, kvs, kvr, kvb, gsum, gsumr, own_e, own_d, st, str_,
    fs, fr, pw, ds, sb1, r1, sum1, sb2, r2, t3, r3, dqs, dqr, dqo, dko, dvo, gko, gvo,
    in_sem, out_sem, ss, rs,
):
    grp = lax.axis_index("grp")
    ctx = lax.axis_index("ctx")
    x_lo, y = lax.div(grp, 4), lax.rem(grp, 4)
    z = lax.div(ctx, 4)
    z_hi, z_lo, low = lax.div(z, 2), lax.rem(z, 2), lax.rem(ctx, 4)
    a = x_lo * 8 + z_lo * 4 + low

    def a_peer(b):
        return {
            "grp": lax.div(b, 8) * 4 + y,
            "ctx": (z_hi * 2 + lax.rem(lax.div(b, 4), 2)) * 4 + lax.rem(b, 4),
        }

    def z_peer(b):
        return {"grp": grp, "ctx": (b * 2 + z_lo) * 4 + low}

    def y_peer(b):
        return {"grp": x_lo * 4 + b, "ctx": ctx}

    a_others = [lax.rem(a + k, 16) for k in range(1, 16)]
    z_others = [lax.rem(z_hi + k, 4) for k in range(1, 4)]
    y_others = [lax.rem(y + k, 4) for k in range(1, 4)]

    def remote(kind, src, dst, device):
        return pltpu.make_async_remote_copy(
            src_ref=src, dst_ref=dst, send_sem=ss.at[kind], recv_sem=rs.at[kind],
            device_id=device, device_id_type=MESH,
        )

    def arrived(kind, dst):
        remote(kind, dst, dst, y_peer(y_others[0])).wait_recv()

    def sent(kind, src):
        remote(kind, src, src, y_peer(y_others[0])).wait_send()

    loads = [
        pltpu.make_async_copy(src, dst, in_sem.at[n])
        for n, (src, dst) in enumerate(
            (
                (pk_hbm, pk), (pv_hbm, pv), (rw_hbm, rw), (mp_hbm, mp),
                (cq_hbm, cq), (go_hbm, go), (ck_hbm, ck), (cv_hbm, cv),
            )
        )
    ]
    for load in loads:
        load.start()

    barrier = pltpu.get_barrier_semaphore()
    for b in a_others:
        pl.semaphore_signal(barrier, inc=1, device_id=a_peer(b), device_id_type=MESH)
    for b in z_others:
        pl.semaphore_signal(barrier, inc=1, device_id=z_peer(b), device_id_type=MESH)
    for b in y_others:
        pl.semaphore_signal(barrier, inc=1, device_id=y_peer(b), device_id_type=MESH)

    for load in loads[:4]:
        load.wait()
    pos = mp[...]
    pos2 = jnp.concatenate([pos, pos], axis=1)
    live = pos < ROWS
    count = jnp.sum(jnp.where(live, 1.0, 0.0), axis=1, keepdims=True)
    reward = rw[...]
    lines = jnp.concatenate(
        [
            pk[...].astype(F32),
            pv[...].astype(F32),
            jnp.broadcast_to(count, (1, WIDTH)),
            jnp.broadcast_to(reward, (1, WIDTH)),
            jnp.zeros((2, WIDTH), F32),
        ],
        axis=0,
    )
    for h in range(HEADS):
        kvs[h] = lines[:, h * DIM : (h + 1) * DIM]

    pl.semaphore_wait(barrier, 21)

    for b in a_others:
        remote(KV, kvs.at[b], kvr.at[a], a_peer(b)).start()
    kvr[a] = kvs[a]

    row = lax.broadcasted_iota(jnp.int32, (ROWS, 2 * SLOTS), 0)
    pick = jnp.where(row == jnp.minimum(pos2, ROWS - 1), 1.0, 0.0).astype(BF16)
    loads[4].wait()
    picked = dot_tn(pick, cq[...])[:SLOTS].astype(BF16)
    loads[5].wait()
    for h in range(HEADS):
        xb[h, 0:SLOTS, :] = picked[:, h * DIM : (h + 1) * DIM]
        xb[h, SLOTS : 2 * SLOTS, :] = go[:, h * DIM : (h + 1) * DIM]

    arrived(KV, kvr.at[pl.ds(0, 15)])
    blocks = kvr[...]
    kvb[y, z_hi, 0, 0:16, :] = blocks[:, 0, :].astype(BF16)
    kvb[y, z_hi, 0, 16:32, :] = blocks[:, 1, :].astype(BF16)
    kvb[y, z_hi, 1, 0:16, :] = blocks[:, 2, :].astype(BF16)
    kvb[y, z_hi, 1, 16:32, :] = blocks[:, 3, :].astype(BF16)
    for b in z_others:
        remote(ZKV, kvb.at[y, z_hi], kvb.at[y, z_hi], z_peer(b)).start()
    mine = lax.broadcasted_iota(jnp.int32, (16, DIM), 0) // 8 == x_lo
    count16 = jnp.sum(jnp.where(mine, blocks[:, 4, :], 0.0), axis=0, keepdims=True)
    reward16 = jnp.sum(jnp.where(mine, blocks[:, 5, :], 0.0), axis=0, keepdims=True)
    gsum[...] = jnp.concatenate([count16, reward16, jnp.zeros((6, DIM), F32)], axis=0)
    for b in z_others:
        remote(ZSUM, gsum, gsumr.at[z_hi], z_peer(b)).start()

    for b in a_others:
        remote(QG, xb.at[b], xbr.at[a], a_peer(b)).start()
    xbr[a] = xb[a]

    def own_scores(h):
        q = xb[h, 0:SLOTS, :]
        g = xb[h, SLOTS : 2 * SLOTS, :]
        s = dot_nt(ck[:, h * DIM : (h + 1) * DIM], jnp.concatenate([q, q], axis=0)) * SCALE2
        d = dot_nt(cv[:, h * DIM : (h + 1) * DIM], jnp.concatenate([g, g], axis=0))
        m = jnp.max(s, axis=0, keepdims=True)
        e = jnp.exp2(s - m)
        own_e[h] = e
        own_d[h] = d
        st[h] = jnp.concatenate(
            [
                m,
                jnp.sum(e, axis=0, keepdims=True),
                jnp.sum(e * d, axis=0, keepdims=True),
                jnp.zeros((5, DIM), F32),
            ],
            axis=0,
        )

    loads[6].wait()
    loads[7].wait()
    for h in range(HEADS // 2):
        own_scores(h)

    arrived(ZKV, kvb.at[0, pl.ds(0, 3)])
    for b in y_others:
        remote(YKV, kvb.at[y], kvb.at[y], y_peer(b)).start()
    for h in range(HEADS // 2, HEADS):
        own_scores(h)
    arrived(ZSUM, gsumr.at[pl.ds(0, 3)])
    total = gsum[...]
    for b in z_others:
        total = total + gsumr[b]
    weight = (reward - total[1:2] / 32.0) * (SLOTS * 32) / total[0:1]
    weight = jnp.where(pos2 < ROWS, weight, 0.0)
    for h in range(HEADS):
        st[h, 3:4, :] = weight
    for b in a_others:
        remote(OWN, st.at[b], str_.at[a], a_peer(b)).start()
    str_[a] = st[a]

    arrived(QG, xbr.at[pl.ds(0, 15)])
    arrived(YKV, kvb.at[pl.ds(0, 3)])
    arrived(OWN, str_.at[pl.ds(0, 15)])
    keys = kvb[:, :, 0].reshape(PROMPT, DIM)
    values = kvb[:, :, 1].reshape(PROMPT, DIM)
    left = lax.broadcasted_iota(jnp.int32, (8, DIM), 1) < SLOTS
    def pair(t, _):
        q = xbr[pl.ds(2 * t, 2), 0:SLOTS, :].reshape(2 * SLOTS, DIM)
        g = xbr[pl.ds(2 * t, 2), SLOTS : 2 * SLOTS, :].reshape(2 * SLOTS, DIM)
        s = dot_nt(keys, q) * SCALE2
        d = dot_nt(values, g)
        mp_ = jnp.max(s, axis=0, keepdims=True)
        e = jnp.exp2(s - mp_)
        lp = jnp.sum(e, axis=0, keepdims=True)
        ip = jnp.sum(e * d, axis=0, keepdims=True)
        stats = jnp.where(left, str_[2 * t], str_[2 * t + 1])
        mo, lo, io, w = stats[0:1], stats[1:2], stats[2:3], stats[3:4]
        m = jnp.maximum(mp_, mo)
        fp = jnp.exp2(mp_ - m)
        fo = jnp.exp2(mo - m)
        inv = 1.0 / (lp * fp + lo * fo)
        inner = (ip * fp + io * fo) * inv
        coef = fp * inv * w
        cols = pl.ds(pl.multiple_of(t * 128, 128), 128)
        p = (e * coef).astype(BF16)
        dsc = (e * (d - inner) * (coef * SCALE)).astype(BF16)
        pw[:, :, cols] = p.reshape(4, 128, 128)
        ds[:, :, cols] = dsc.reshape(4, 128, 128)
        final = jnp.concatenate([m, inv, inner, jnp.zeros((5, DIM), F32)], axis=0)
        fs[2 * t] = final
        fs[2 * t + 1] = final
        return 0

    lax.fori_loop(0, 8, pair, 0, unroll=2)

    q_all = xbr[:, 0:SLOTS, :].reshape(16 * SLOTS, DIM)
    g_all = xbr[:, SLOTS : 2 * SLOTS, :].reshape(16 * SLOTS, DIM)
    for b in y_others + [y]:
        grad_k = dot_nn(ds[b], q_all)
        grad_v = dot_nn(pw[b], g_all)
        if b is not y:
            sb1[b, 0] = grad_k.astype(BF16)
            sb1[b, 1] = grad_v.astype(BF16)
            remote(RS1, sb1.at[b], r1.at[y], y_peer(b)).start()
    for b in a_others:
        remote(FIN, fs.at[b], fr.at[a], a_peer(b)).start()
    fr[a] = fs[a]
    for t in range(8):
        grad_q = dot_tn(ds[:, :, t * 128 : (t + 1) * 128].reshape(PROMPT, 2 * SLOTS), keys)
        dqs[2 * t] = grad_q[:SLOTS].astype(BF16)
        dqs[2 * t + 1] = grad_q[SLOTS:].astype(BF16)
    for b in a_others:
        remote(DQ, dqs.at[b], dqr.at[a], a_peer(b)).start()
    dqr[a] = dqs[a]

    arrived(RS1, r1.at[pl.ds(0, 3)])
    for b in y_others:
        grad_k = grad_k + r1[b, 0].astype(F32)
        grad_v = grad_v + r1[b, 1].astype(F32)
    for b in range(4):
        sum1[b, 0] = grad_k[b * 32 : (b + 1) * 32]
        sum1[b, 1] = grad_v[b * 32 : (b + 1) * 32]
        sb2[b, 0] = grad_k[b * 32 : (b + 1) * 32].astype(BF16)
        sb2[b, 1] = grad_v[b * 32 : (b + 1) * 32].astype(BF16)
    for b in z_others:
        remote(RS2, sb2.at[b], r2.at[z_hi], z_peer(b)).start()

    arrived(FIN, fr.at[pl.ds(0, 15)])
    arrived(DQ, dqr.at[pl.ds(0, 15)])
    here = left == (lax.rem(a, 2) == 0)
    nothing = jnp.zeros((SLOTS, DIM), BF16)
    for h in range(HEADS):
        cols = slice(h * DIM, (h + 1) * DIM)
        fin = fr[h]
        fin = jnp.where(here, fin, jnp.concatenate([fin[:, SLOTS:], fin[:, :SLOTS]], axis=1))
        m, inv, inner = fin[0:1], fin[1:2], fin[2:3]
        coef = jnp.exp2(st[h, 0:1, :] - m) * inv * weight
        e = own_e[h]
        p = (e * coef).astype(BF16)
        dsc = (e * (own_d[h] - inner) * (coef * SCALE)).astype(BF16)
        dvo[:, cols] = dot_nn(p, jnp.concatenate([xb[h, SLOTS:, :], nothing], axis=0)).astype(BF16)
        dko[:, cols] = dot_nn(dsc, jnp.concatenate([xb[h, :SLOTS, :], nothing], axis=0)).astype(BF16)
        dqo[:, cols] = (dot_tn(dsc, ck[:, cols])[:SLOTS] + dqr[h].astype(F32)).astype(BF16)
    stores = [
        pltpu.make_async_copy(src, dst, out_sem.at[n])
        for n, (src, dst) in enumerate(
            ((dqo, dq_hbm), (dko, dk_hbm), (dvo, dv_hbm), (gko, gk_hbm), (gvo, gv_hbm))
        )
    ]
    for store in stores[:3]:
        store.start()

    arrived(RS2, r2.at[pl.ds(0, 3)])
    line = lax.broadcasted_iota(jnp.int32, (16, 8, DIM), 1)
    lines = jnp.zeros((16, 8, DIM), F32)
    for kv in range(2):
        part = sum1[z_hi, kv]
        for b in z_others:
            part = part + r2[b, kv].astype(F32)
        for r in range(2):
            lines = jnp.where(line == kv * 2 + r, part[r * 16 : (r + 1) * 16][:, None, :], lines)
    t3[...] = lines
    for b in a_others:
        remote(RS3, t3.at[b], r3.at[a], a_peer(b)).start()
    r3[a] = t3[a]
    arrived(RS3, r3.at[pl.ds(0, 15)])
    for h in range(HEADS):
        cols = slice(h * DIM, (h + 1) * DIM)
        gko[:, cols] = r3[h, 0:2, :].astype(BF16)
        gvo[:, cols] = r3[h, 2:4, :].astype(BF16)

    for store in stores[3:]:
        store.start()

    sent(KV, kvs.at[pl.ds(0, 15)])
    sent(QG, xb.at[pl.ds(0, 15)])
    sent(ZKV, kvb.at[0, pl.ds(0, 3)])
    sent(ZSUM, gsumr.at[pl.ds(0, 3)])
    sent(YKV, kvb.at[pl.ds(0, 3)])
    sent(OWN, st.at[pl.ds(0, 15)])
    sent(FIN, fs.at[pl.ds(0, 15)])
    sent(DQ, dqs.at[pl.ds(0, 15)])
    sent(RS1, sb1.at[pl.ds(0, 3)])
    sent(RS2, sb2.at[pl.ds(0, 3)])
    sent(RS3, t3.at[pl.ds(0, 15)])
    for store in stores:
        store.wait()


def store_all(*refs):
    sources, targets, held, sem = refs[:5], refs[5:10], refs[10:15], refs[15]
    parts = []
    for n in range(5):
        rows = sources[n].shape[0]
        step = min(rows, SLOTS)
        for first in range(0, rows, step):
            parts.append((n, pl.ds(first, step)))
    loads = [
        pltpu.make_async_copy(sources[n].at[span], held[n].at[span], sem.at[0, p])
        for p, (n, span) in enumerate(parts)
    ]
    stores = [
        pltpu.make_async_copy(held[n].at[span], targets[n].at[span], sem.at[1, p])
        for p, (n, span) in enumerate(parts)
    ]
    for load in loads:
        load.start()
    for load, store in zip(loads, stores):
        load.wait()
        store.start()
    for store in stores:
        store.wait()


def shards(prompt_k, prompt_v, comp_q, comp_k, comp_v, grad_out, rewards, mask_pos):
    hbm = pl.BlockSpec(memory_space=pltpu.HBM)
    V = pltpu.VMEM
    grads = pl.pallas_call(
        kernel,
        out_shape=(
            jax.ShapeDtypeStruct((SLOTS, WIDTH), BF16),
            jax.ShapeDtypeStruct((ROWS, WIDTH), BF16),
            jax.ShapeDtypeStruct((ROWS, WIDTH), BF16),
            jax.ShapeDtypeStruct((2, WIDTH), BF16),
            jax.ShapeDtypeStruct((2, WIDTH), BF16),
        ),
        in_specs=[hbm] * 8,
        out_specs=(hbm,) * 5,
        scratch_shapes=[
            V((2, WIDTH), BF16),
            V((2, WIDTH), BF16),
            V((1, 1), F32),
            V((1, SLOTS), jnp.int32),
            V((ROWS, WIDTH), BF16),
            V((ROWS, WIDTH), BF16),
            V((ROWS, WIDTH), BF16),
            V((SLOTS, WIDTH), BF16),
            V((16, 128, DIM), BF16),
            V((16, 128, DIM), BF16),
            V((16, 8, DIM), F32),
            V((16, 8, DIM), F32),
            V((4, 4, 2, 32, DIM), BF16),
            V((8, DIM), F32),
            V((4, 8, DIM), F32),
            V((16, 128, DIM), F32),
            V((16, 128, DIM), F32),
            V((16, 8, DIM), F32),
            V((16, 8, DIM), F32),
            V((16, 8, DIM), F32),
            V((16, 8, DIM), F32),
            V((4, 128, 16 * SLOTS), BF16),
            V((4, 128, 16 * SLOTS), BF16),
            V((4, 2, 128, DIM), BF16),
            V((4, 2, 128, DIM), BF16),
            V((4, 2, 32, DIM), F32),
            V((4, 2, 32, DIM), BF16),
            V((4, 2, 32, DIM), BF16),
            V((16, 8, DIM), F32),
            V((16, 8, DIM), F32),
            V((16, SLOTS, DIM), BF16),
            V((16, SLOTS, DIM), BF16),
            V((SLOTS, WIDTH), BF16),
            V((ROWS, WIDTH), BF16),
            V((ROWS, WIDTH), BF16),
            V((2, WIDTH), BF16),
            V((2, WIDTH), BF16),
            pltpu.SemaphoreType.DMA((8,)),
            pltpu.SemaphoreType.DMA((5,)),
            pltpu.SemaphoreType.DMA((KINDS,)),
            pltpu.SemaphoreType.DMA((KINDS,)),
        ],
        compiler_params=pltpu.CompilerParams(
            collective_id=0, has_side_effects=True, vmem_limit_bytes=60 * 1024 * 1024
        ),
    )(
        prompt_k, prompt_v, rewards, mask_pos[0], comp_q[0, 0], comp_k[0, 0], comp_v[0, 0],
        grad_out[0, 0],
    )
    dq, dk, dv, gk, gv = pl.pallas_call(
        store_all,
        out_shape=[jax.ShapeDtypeStruct(grad.shape, BF16) for grad in grads],
        in_specs=[hbm] * 5,
        out_specs=[hbm] * 5,
        scratch_shapes=[V(grad.shape, BF16) for grad in grads] + [pltpu.SemaphoreType.DMA((2, 7))],
        compiler_params=pltpu.CompilerParams(vmem_limit_bytes=60 * 1024 * 1024),
    )(*grads)
    return dq[None, None], dk[None, None], dv[None, None], gk, gv


def solution(mesh):
    wide = P("grp", "ctx", None, None)
    rows = P(("grp", "ctx"), None)
    return jax.shard_map(
        shards,
        mesh=mesh,
        in_specs=(rows, rows, wide, wide, wide, wide, P("grp", "ctx"), P("grp", "ctx", None)),
        out_specs=(wide, wide, wide, rows, rows),
        check_vma=False,
    )
```

time: 1010 us -> 47.3 us (0.05)
  waiting for transfers between devices: 735 us -> 0 us
  blocking collectives: 212 us -> 0 us
  Pallas kernels: 0 us -> 45.9 us
  local copies, waits for them, and re-layouts: 26.5 us -> 0 us
  matrix products: 18.7 us -> 0 us
  between operations: 16.3 us -> 1.29 us
    all_gather x2 -> x0, waiting for transfers between devices: 733 us -> none  [the longest x1 400 us: shards(): lax.all_gather(prompt_v, ('grp', 'ctx'), axis=0, tiled=True)]
    unnamed x1 -> x0, blocking collectives: 142 us -> none
    psum x1 -> x0, blocking collectives: 69.6 us -> none  [shards(): group_count, reward_total = lax.psum((masked_count, rewards[0, 0]), 'ctx')]
    pallas_call x0 -> x2, Pallas kernels: none -> 45.9 us  [the longest x1 43.8 us: shards(): pl.pallas_call(kernel, out_shape=(jax.ShapeDtypeStruct((SLOTS, WIDTH), BF...]
    dot_general x12 -> x0, matrix products: 18.7 us -> none  [output_products(): return jnp.einsum(form, left, right, preferred_element_type=jnp.float32)]
    reshape x4 -> x0, local copies, waits for them, and re-layouts: 18.3 us -> none  [the longest x1 5.41 us: attention_grads(): gradient_context_value.reshape(-1, features)]
  transfers between devices with their start and end apart: 2 -> 0, of which waited for: 2 -> 0; matrix products, arithmetic and copies ran while one was open for 1% -> 0% of each run, Pallas kernels for 0% -> 0%
where the time goes in v1:
time: 47.3 us; the launch traced here: 47.2 us
  Pallas kernels  45.9 us (97%)
  between operations  1.29 us (3%)
    pallas_call x1, Pallas kernels, shards(): pl.pallas_call(kernel, out_shape=(jax.ShapeDtypeStruct((SLOTS, WIDTH), BF...  43.8 us
    pallas_call x1, Pallas kernels, shards(): pl.pallas_call(store_all, out_shape=[jax.ShapeDtypeStruct(grad.shape, BF1...  2.12 us

profile of v1, /device:TPU:1, one launch (start us, length us, event | category | flops | bytes accessed | tf_op | source)
XLA Modules:
  0.0 47.2 jit_solution(917973767334730362)
XLA Ops:
  1.3 43.8 %shard_map.119 = (bf16[64,2048]{1,0:T(8,128)(2,1)}, bf16[128,2048]{1,0:T(8,128)(2,1)}, bf16[128,2048]{1,0:T(8,128)(2,1)}, bf16[2,2048]{1,0:T(2,128)(2,1)}, bf16[2,2048]{1,0:T(2,128)(2,1)}) custom-call(bf16[2,2048]{1,0:T(2,128)(2,1)} %pk_hbm.1, bf16[2,2048]{1,0:T(2,128)(2,1)} %pv_hbm.1, f32[1,1]{1,0:T(1,128)S(6)} %copy.13.rw_hbm, s32[1,64]{1,0:T(1,128)} %bitcast.12, ...), custom_call_target="tpu_custom_call" | custom-call | tf_op jit(solution)/shard_map/pallas_call | solution.py:349
  45.1 2.1 %shard_map.120 = (bf16[64,2048]{1,0:T(8,128)(2,1)}, bf16[128,2048]{1,0:T(8,128)(2,1)}, bf16[128,2048]{1,0:T(8,128)(2,1)}, bf16[2,2048]{1,0:T(2,128)(2,1)}, bf16[2,2048]{1,0:T(2,128)(2,1)}) custom-call(bf16[64,2048]{1,0:T(8,128)(2,1)} %get-tuple-element.15.refs_0_, bf16[128,2048]{1,0:T(8,128)(2,1)} %get-tuple-element.16.refs_1_, ...), custom_call_target="tpu_custom_call" | custom-call | tf_op jit(solution)/shard_map/pallas_call | solution.py:410

commit v2 on v1

--- a/solution.py
+++ b/solution.py
@@ -17,7 +17,7 @@
 SCALE2 = SCALE * 1.4426950408889634
 MESH = pl.DeviceIdType.MESH
 
-KV, QG, ZKV, ZSUM, YKV, OWN, FIN, DQ, RS1, RS2, RS3, KINDS = range(12)
+KV, QG, ZKV, ZSUM, XSUM, YKV, OWN, FIN, DQ, RS1, RS2, RS3, KINDS = range(13)
 
 
 def dot_nt(a, b):
@@ -35,32 +35,40 @@
 def kernel(
     pk_hbm, pv_hbm, rw_hbm, mp_hbm, cq_hbm, ck_hbm, cv_hbm, go_hbm,
     dq_hbm, dk_hbm, dv_hbm, gk_hbm, gv_hbm,
-    pk, pv, rw, mp, cq, ck, cv, go, xb, xbr, kvs, kvr, kvb, gsum, gsumr, own_e, own_d, st, str_,
+    pk, pv, rw, mp, cq, ck, cv, go, xb, xbr, kvs, kvr, kvb, gsum, gsumr, gsum2, gsumx, own_e, own_d, st, str_,
     fs, fr, pw, ds, sb1, r1, sum1, sb2, r2, t3, r3, dqs, dqr, dqo, dko, dvo, gko, gvo,
     in_sem, out_sem, ss, rs,
 ):
     grp = lax.axis_index("grp")
     ctx = lax.axis_index("ctx")
-    x_lo, y = lax.div(grp, 4), lax.rem(grp, 4)
-    z = lax.div(ctx, 4)
-    z_hi, z_lo, low = lax.div(z, 2), lax.rem(z, 2), lax.rem(ctx, 4)
-    a = x_lo * 8 + z_lo * 4 + low
-
-    def a_peer(b):
+    x_lo, y_hi, y_lo = lax.div(grp, 4), lax.rem(lax.div(grp, 2), 2), lax.rem(grp, 2)
+    z_hi, z_lo = lax.div(ctx, 8), lax.rem(lax.div(ctx, 4), 2)
+    x_hi, core = lax.rem(lax.div(ctx, 2), 2), lax.rem(ctx, 2)
+    a = x_lo * 8 + y_lo * 4 + z_lo * 2 + core
+    w = x_hi * 2 + y_hi
+
+    def device(x_lo, x_hi, y_lo, y_hi, z_lo, z_hi, core):
         return {
-            "grp": lax.div(b, 8) * 4 + y,
-            "ctx": (z_hi * 2 + lax.rem(lax.div(b, 4), 2)) * 4 + lax.rem(b, 4),
+            "grp": x_lo * 4 + y_hi * 2 + y_lo,
+            "ctx": (z_hi * 2 + z_lo) * 4 + x_hi * 2 + core,
         }
 
-    def z_peer(b):
-        return {"grp": grp, "ctx": (b * 2 + z_lo) * 4 + low}
-
-    def y_peer(b):
-        return {"grp": x_lo * 4 + b, "ctx": ctx}
-
+    def a_peer(i):
+        return device(
+            lax.div(i, 8), x_hi, lax.rem(lax.div(i, 4), 2), y_hi,
+            lax.rem(lax.div(i, 2), 2), z_hi, lax.rem(i, 2),
+        )
+
+    def z_peer(i):
+        return device(x_lo, x_hi, y_lo, y_hi, z_lo, i, core)
+
+    def w_peer(i):
+        return device(x_lo, lax.div(i, 2), y_lo, lax.rem(i, 2), z_lo, z_hi, core)
+
+    x_peer = device(x_lo, 1 - x_hi, y_lo, y_hi, z_lo, z_hi, core)
     a_others = [lax.rem(a + k, 16) for k in range(1, 16)]
     z_others = [lax.rem(z_hi + k, 4) for k in range(1, 4)]
-    y_others = [lax.rem(y + k, 4) for k in range(1, 4)]
+    w_others = [lax.rem(w + k, 4) for k in range(1, 4)]
 
     def remote(kind, src, dst, device):
         return pltpu.make_async_remote_copy(
@@ -69,10 +77,10 @@
         )
 
     def arrived(kind, dst):
-        remote(kind, dst, dst, y_peer(y_others[0])).wait_recv()
+        remote(kind, dst, dst, w_peer(w_others[0])).wait_recv()
 
     def sent(kind, src):
-        remote(kind, src, src, y_peer(y_others[0])).wait_send()
+        remote(kind, src, src, w_peer(w_others[0])).wait_send()
 
     loads = [
         pltpu.make_async_copy(src, dst, in_sem.at[n])
@@ -91,8 +99,8 @@
         pl.semaphore_signal(barrier, inc=1, device_id=a_peer(b), device_id_type=MESH)
     for b in z_others:
         pl.semaphore_signal(barrier, inc=1, device_id=z_peer(b), device_id_type=MESH)
-    for b in y_others:
-        pl.semaphore_signal(barrier, inc=1, device_id=y_peer(b), device_id_type=MESH)
+    for b in w_others:
+        pl.semaphore_signal(barrier, inc=1, device_id=w_peer(b), device_id_type=MESH)
 
     for load in loads[:4]:
         load.wait()
@@ -131,13 +139,13 @@
 
     arrived(KV, kvr.at[pl.ds(0, 15)])
     blocks = kvr[...]
-    kvb[y, z_hi, 0, 0:16, :] = blocks[:, 0, :].astype(BF16)
-    kvb[y, z_hi, 0, 16:32, :] = blocks[:, 1, :].astype(BF16)
-    kvb[y, z_hi, 1, 0:16, :] = blocks[:, 2, :].astype(BF16)
-    kvb[y, z_hi, 1, 16:32, :] = blocks[:, 3, :].astype(BF16)
+    kvb[w, z_hi, 0, 0:16, :] = blocks[:, 0, :].astype(BF16)
+    kvb[w, z_hi, 0, 16:32, :] = blocks[:, 1, :].astype(BF16)
+    kvb[w, z_hi, 1, 0:16, :] = blocks[:, 2, :].astype(BF16)
+    kvb[w, z_hi, 1, 16:32, :] = blocks[:, 3, :].astype(BF16)
     for b in z_others:
-        remote(ZKV, kvb.at[y, z_hi], kvb.at[y, z_hi], z_peer(b)).start()
-    mine = lax.broadcasted_iota(jnp.int32, (16, DIM), 0) // 8 == x_lo
+        remote(ZKV, kvb.at[w, z_hi], kvb.at[w, z_hi], z_peer(b)).start()
+    mine = lax.broadcasted_iota(jnp.int32, (16, DIM), 0) // 4 == lax.div(a, 4)
     count16 = jnp.sum(jnp.where(mine, blocks[:, 4, :], 0.0), axis=0, keepdims=True)
     reward16 = jnp.sum(jnp.where(mine, blocks[:, 5, :], 0.0), axis=0, keepdims=True)
     gsum[...] = jnp.concatenate([count16, reward16, jnp.zeros((6, DIM), F32)], axis=0)
@@ -173,14 +181,18 @@
         own_scores(h)
 
     arrived(ZKV, kvb.at[0, pl.ds(0, 3)])
-    for b in y_others:
-        remote(YKV, kvb.at[y], kvb.at[y], y_peer(b)).start()
-    for h in range(HEADS // 2, HEADS):
-        own_scores(h)
+    for b in w_others:
+        remote(YKV, kvb.at[w], kvb.at[w], w_peer(b)).start()
     arrived(ZSUM, gsumr.at[pl.ds(0, 3)])
     total = gsum[...]
     for b in z_others:
         total = total + gsumr[b]
+    gsum2[...] = total
+    remote(XSUM, gsum2, gsumx, x_peer).start()
+    for h in range(HEADS // 2, HEADS):
+        own_scores(h)
+    arrived(XSUM, gsumx)
+    total = total + gsumx[...]
     weight = (reward - total[1:2] / 32.0) * (SLOTS * 32) / total[0:1]
     weight = jnp.where(pos2 < ROWS, weight, 0.0)
     for h in range(HEADS):
@@ -205,13 +217,13 @@
         lp = jnp.sum(e, axis=0, keepdims=True)
         ip = jnp.sum(e * d, axis=0, keepdims=True)
         stats = jnp.where(left, str_[2 * t], str_[2 * t + 1])
-        mo, lo, io, w = stats[0:1], stats[1:2], stats[2:3], stats[3:4]
+        mo, lo, io, tw = stats[0:1], stats[1:2], stats[2:3], stats[3:4]
         m = jnp.maximum(mp_, mo)
         fp = jnp.exp2(mp_ - m)
         fo = jnp.exp2(mo - m)
         inv = 1.0 / (lp * fp + lo * fo)
         inner = (ip * fp + io * fo) * inv
-        coef = fp * inv * w
+        coef = fp * inv * tw
         cols = pl.ds(pl.multiple_of(t * 128, 128), 128)
         p = (e * coef).astype(BF16)
         dsc = (e * (d - inner) * (coef * SCALE)).astype(BF16)
@@ -226,13 +238,13 @@
 
     q_all = xbr[:, 0:SLOTS, :].reshape(16 * SLOTS, DIM)
     g_all = xbr[:, SLOTS : 2 * SLOTS, :].reshape(16 * SLOTS, DIM)
-    for b in y_others + [y]:
+    for b in w_others + [w]:
         grad_k = dot_nn(ds[b], q_all)
         grad_v = dot_nn(pw[b], g_all)
-        if b is not y:
+        if b is not w:
             sb1[b, 0] = grad_k.astype(BF16)
             sb1[b, 1] = grad_v.astype(BF16)
-            remote(RS1, sb1.at[b], r1.at[y], y_peer(b)).start()
+            remote(RS1, sb1.at[b], r1.at[w], w_peer(b)).start()
     for b in a_others:
         remote(FIN, fs.at[b], fr.at[a], a_peer(b)).start()
     fr[a] = fs[a]
@@ -245,7 +257,7 @@
     dqr[a] = dqs[a]
 
     arrived(RS1, r1.at[pl.ds(0, 3)])
-    for b in y_others:
+    for b in w_others:
         grad_k = grad_k + r1[b, 0].astype(F32)
         grad_v = grad_v + r1[b, 1].astype(F32)
     for b in range(4):
@@ -307,6 +319,7 @@
     sent(QG, xb.at[pl.ds(0, 15)])
     sent(ZKV, kvb.at[0, pl.ds(0, 3)])
     sent(ZSUM, gsumr.at[pl.ds(0, 3)])
+    sent(XSUM, gsum2)
     sent(YKV, kvb.at[pl.ds(0, 3)])
     sent(OWN, st.at[pl.ds(0, 15)])
     sent(FIN, fs.at[pl.ds(0, 15)])
@@ -373,6 +386,8 @@
             V((4, 4, 2, 32, DIM), BF16),
             V((8, DIM), F32),
             V((4, 8, DIM), F32),
+            V((8, DIM), F32),
+            V((8, DIM), F32),
             V((16, 128, DIM), F32),
             V((16, 128, DIM), F32),
             V((16, 8, DIM), F32),

time: 47.3 us -> 54 us (1.14)
  Pallas kernels: 45.9 us -> 52.6 us
    pallas_call x1, Pallas kernels: 43.8 us -> 50.5 us  [shards(): pl.pallas_call(kernel, out_shape=(jax.ShapeDtypeStruct((SLOTS, WIDTH), BF...]
where the time goes in v2:
time: 54 us; the launch traced here: 53.9 us
  Pallas kernels  52.6 us (97%)
  between operations  1.29 us (2%)
    pallas_call x1, Pallas kernels, shards(): pl.pallas_call(kernel, out_shape=(jax.ShapeDtypeStruct((SLOTS, WIDTH), BF...  50.5 us
    pallas_call x1, Pallas kernels, shards(): pl.pallas_call(store_all, out_shape=[jax.ShapeDtypeStruct(grad.shape, BF1...  2.12 us

profile of v2, /device:TPU:1, one launch (start us, length us, event | category | flops | bytes accessed | tf_op | source)
XLA Modules:
  0.0 53.9 jit_solution(6657516246623080545)
XLA Ops:
  1.3 50.5 %shard_map.119 = (bf16[64,2048]{1,0:T(8,128)(2,1)}, bf16[128,2048]{1,0:T(8,128)(2,1)}, bf16[128,2048]{1,0:T(8,128)(2,1)}, bf16[2,2048]{1,0:T(2,128)(2,1)}, bf16[2,2048]{1,0:T(2,128)(2,1)}) custom-call(bf16[2,2048]{1,0:T(2,128)(2,1)} %pk_hbm.1, bf16[2,2048]{1,0:T(2,128)(2,1)} %pv_hbm.1, f32[1,1]{1,0:T(1,128)S(6)} %copy.13.rw_hbm, s32[1,64]{1,0:T(1,128)} %bitcast.12, ...), custom_call_target="tpu_custom_call" | custom-call | tf_op jit(solution)/shard_map/pallas_call | solution.py:362
  51.7 2.1 %shard_map.120 = (bf16[64,2048]{1,0:T(8,128)(2,1)}, bf16[128,2048]{1,0:T(8,128)(2,1)}, bf16[128,2048]{1,0:T(8,128)(2,1)}, bf16[2,2048]{1,0:T(2,128)(2,1)}, bf16[2,2048]{1,0:T(2,128)(2,1)}) custom-call(bf16[64,2048]{1,0:T(8,128)(2,1)} %get-tuple-element.15.refs_0_, bf16[128,2048]{1,0:T(8,128)(2,1)} %get-tuple-element.16.refs_1_, ...), custom_call_target="tpu_custom_call" | custom-call | tf_op jit(solution)/shard_map/pallas_call | solution.py:425

commit v3 on v1

--- a/solution.py
+++ b/solution.py
@@ -17,7 +17,9 @@
 SCALE2 = SCALE * 1.4426950408889634
 MESH = pl.DeviceIdType.MESH
 
-KV, QG, ZKV, ZSUM, YKV, OWN, FIN, DQ, RS1, RS2, RS3, KINDS = range(12)
+(
+    KV, QUERY, GRAD, ZK, ZV, ZSUM, YK, YV, OWN, FIN, DQ, YSUM_K, YSUM_V, ZSUM_K, ZSUM_V, OUT, KINDS
+) = range(17)
 
 
 def dot_nt(a, b):
@@ -35,21 +37,22 @@
 def kernel(
     pk_hbm, pv_hbm, rw_hbm, mp_hbm, cq_hbm, ck_hbm, cv_hbm, go_hbm,
     dq_hbm, dk_hbm, dv_hbm, gk_hbm, gv_hbm,
-    pk, pv, rw, mp, cq, ck, cv, go, xb, xbr, kvs, kvr, kvb, gsum, gsumr, own_e, own_d, st, str_,
-    fs, fr, pw, ds, sb1, r1, sum1, sb2, r2, t3, r3, dqs, dqr, dqo, dko, dvo, gko, gvo,
-    in_sem, out_sem, ss, rs,
+    pk, pv, rw, mp, cq, ck, cv, go, xq, xqr, xg, xgr, kvs, kvr, kb, vb, gsum, gsumr, own_e, own_d, st, str_,
+    fs, fr, exps, prods, part, pw, ds,
+    sbk, sbv, rk, rv, hk, hv, szk, szv, rzk, rzv, t3, r3, dqs, dqr, dqo, dko, dvo, gko, gvo,
+    in_sem, out_sem, ss, rs, ry,
 ):
     grp = lax.axis_index("grp")
     ctx = lax.axis_index("ctx")
     x_lo, y = lax.div(grp, 4), lax.rem(grp, 4)
     z = lax.div(ctx, 4)
     z_hi, z_lo, low = lax.div(z, 2), lax.rem(z, 2), lax.rem(ctx, 4)
-    a = x_lo * 8 + z_lo * 4 + low
+    a = z_lo * 8 + x_lo * 4 + low
 
     def a_peer(b):
         return {
-            "grp": lax.div(b, 8) * 4 + y,
-            "ctx": (z_hi * 2 + lax.rem(lax.div(b, 4), 2)) * 4 + lax.rem(b, 4),
+            "grp": lax.rem(lax.div(b, 4), 2) * 4 + y,
+            "ctx": (z_hi * 2 + lax.div(b, 8)) * 4 + lax.rem(b, 4),
         }
 
     def z_peer(b):
@@ -58,7 +61,8 @@
     def y_peer(b):
         return {"grp": x_lo * 4 + b, "ctx": ctx}
 
-    a_others = [lax.rem(a + k, 16) for k in range(1, 16)]
+    a_others = [z_lo * 8 + lax.rem(a + k, 8) for k in range(1, 8)]
+    a_others += [(1 - z_lo) * 8 + lax.rem(a + k, 8) for k in range(8)]
     z_others = [lax.rem(z_hi + k, 4) for k in range(1, 4)]
     y_others = [lax.rem(y + k, 4) for k in range(1, 4)]
 
@@ -66,6 +70,12 @@
         return pltpu.make_async_remote_copy(
             src_ref=src, dst_ref=dst, send_sem=ss.at[kind], recv_sem=rs.at[kind],
             device_id=device, device_id_type=MESH,
+        )
+
+    def along_y(kv, ref, row, b):
+        return pltpu.make_async_remote_copy(
+            src_ref=ref.at[row], dst_ref=ref.at[row], send_sem=ss.at[YK + kv],
+            recv_sem=ry.at[kv, row], device_id=y_peer(b), device_id_type=MESH,
         )
 
     def arrived(kind, dst):
@@ -124,33 +134,38 @@
     pick = jnp.where(row == jnp.minimum(pos2, ROWS - 1), 1.0, 0.0).astype(BF16)
     loads[4].wait()
     picked = dot_tn(pick, cq[...])[:SLOTS].astype(BF16)
+    for h in range(HEADS):
+        xq[h] = picked[:, h * DIM : (h + 1) * DIM]
+    for b in a_others:
+        remote(QUERY, xq.at[b], xqr.at[a], a_peer(b)).start()
+    xqr[a] = xq[a]
     loads[5].wait()
     for h in range(HEADS):
-        xb[h, 0:SLOTS, :] = picked[:, h * DIM : (h + 1) * DIM]
-        xb[h, SLOTS : 2 * SLOTS, :] = go[:, h * DIM : (h + 1) * DIM]
+        xg[h] = go[:, h * DIM : (h + 1) * DIM]
 
     arrived(KV, kvr.at[pl.ds(0, 15)])
     blocks = kvr[...]
-    kvb[y, z_hi, 0, 0:16, :] = blocks[:, 0, :].astype(BF16)
-    kvb[y, z_hi, 0, 16:32, :] = blocks[:, 1, :].astype(BF16)
-    kvb[y, z_hi, 1, 0:16, :] = blocks[:, 2, :].astype(BF16)
-    kvb[y, z_hi, 1, 16:32, :] = blocks[:, 3, :].astype(BF16)
+    kb[y, z_hi, 0:16, :] = blocks[:, 0, :].astype(BF16)
+    kb[y, z_hi, 16:32, :] = blocks[:, 1, :].astype(BF16)
     for b in z_others:
-        remote(ZKV, kvb.at[y, z_hi], kvb.at[y, z_hi], z_peer(b)).start()
-    mine = lax.broadcasted_iota(jnp.int32, (16, DIM), 0) // 8 == x_lo
+        remote(ZK, kb.at[y, z_hi], kb.at[y, z_hi], z_peer(b)).start()
+    vb[y, z_hi, 0:16, :] = blocks[:, 2, :].astype(BF16)
+    vb[y, z_hi, 16:32, :] = blocks[:, 3, :].astype(BF16)
+    for b in z_others:
+        remote(ZV, vb.at[y, z_hi], vb.at[y, z_hi], z_peer(b)).start()
+    mine = lax.broadcasted_iota(jnp.int32, (16, DIM), 0) // 4 % 2 == x_lo
     count16 = jnp.sum(jnp.where(mine, blocks[:, 4, :], 0.0), axis=0, keepdims=True)
     reward16 = jnp.sum(jnp.where(mine, blocks[:, 5, :], 0.0), axis=0, keepdims=True)
     gsum[...] = jnp.concatenate([count16, reward16, jnp.zeros((6, DIM), F32)], axis=0)
     for b in z_others:
         remote(ZSUM, gsum, gsumr.at[z_hi], z_peer(b)).start()
-
-    for b in a_others:
-        remote(QG, xb.at[b], xbr.at[a], a_peer(b)).start()
-    xbr[a] = xb[a]
+    for b in a_others:
+        remote(GRAD, xg.at[b], xgr.at[a], a_peer(b)).start()
+    xgr[a] = xg[a]
 
     def own_scores(h):
-        q = xb[h, 0:SLOTS, :]
-        g = xb[h, SLOTS : 2 * SLOTS, :]
+        q = xq[h]
+        g = xg[h]
         s = dot_nt(ck[:, h * DIM : (h + 1) * DIM], jnp.concatenate([q, q], axis=0)) * SCALE2
         d = dot_nt(cv[:, h * DIM : (h + 1) * DIM], jnp.concatenate([g, g], axis=0))
         m = jnp.max(s, axis=0, keepdims=True)
@@ -169,13 +184,16 @@
 
     loads[6].wait()
     loads[7].wait()
-    for h in range(HEADS // 2):
+    for h in range(4):
         own_scores(h)
 
-    arrived(ZKV, kvb.at[0, pl.ds(0, 3)])
+    arrived(ZK, kb.at[0, pl.ds(0, 3)])
     for b in y_others:
-        remote(YKV, kvb.at[y], kvb.at[y], y_peer(b)).start()
-    for h in range(HEADS // 2, HEADS):
+        along_y(0, kb, y, b).start()
+    arrived(ZV, vb.at[0, pl.ds(0, 3)])
+    for b in y_others:
+        along_y(1, vb, y, b).start()
+    for h in range(4, HEADS):
         own_scores(h)
     arrived(ZSUM, gsumr.at[pl.ds(0, 3)])
     total = gsum[...]
@@ -189,50 +207,85 @@
         remote(OWN, st.at[b], str_.at[a], a_peer(b)).start()
     str_[a] = st[a]
 
-    arrived(QG, xbr.at[pl.ds(0, 15)])
-    arrived(YKV, kvb.at[pl.ds(0, 3)])
+    def key_block(b):
+        block = kb[b].reshape(128, DIM)
+        for n in range(4):
+            cols = slice(n * 256, (n + 1) * 256)
+            s = dot_nt(block, xqr[4 * n : 4 * n + 4].reshape(256, DIM)) * SCALE2
+            m = jnp.max(s, axis=0, keepdims=True)
+            e = jnp.exp2(s - m)
+            exps[b, :, cols] = e
+            part[b, 0:1, cols] = m
+            part[b, 1:2, cols] = jnp.sum(e, axis=0, keepdims=True)
+
+    def value_block(b):
+        block = vb[b].reshape(128, DIM)
+        for n in range(4):
+            cols = slice(n * 256, (n + 1) * 256)
+            d = dot_nt(block, xgr[4 * n : 4 * n + 4].reshape(256, DIM)) * SCALE
+            prods[b, :, cols] = d
+            part[b, 2:3, cols] = jnp.sum(exps[b, :, cols] * d, axis=0, keepdims=True)
+
+    near_first = [y_others[0], y_others[2], y_others[1]]
+    far_first = [y_others[1], y_others[0], y_others[2]]
+    arrived(QUERY, xqr.at[pl.ds(0, 15)])
+    key_block(y)
+    for b in near_first:
+        along_y(0, kb, b, b).wait_recv()
+        key_block(b)
+    arrived(GRAD, xgr.at[pl.ds(0, 15)])
+    value_block(y)
+    for b in near_first:
+        along_y(1, vb, b, b).wait_recv()
+        value_block(b)
+
     arrived(OWN, str_.at[pl.ds(0, 15)])
-    keys = kvb[:, :, 0].reshape(PROMPT, DIM)
-    values = kvb[:, :, 1].reshape(PROMPT, DIM)
     left = lax.broadcasted_iota(jnp.int32, (8, DIM), 1) < SLOTS
-    def pair(t, _):
-        q = xbr[pl.ds(2 * t, 2), 0:SLOTS, :].reshape(2 * SLOTS, DIM)
-        g = xbr[pl.ds(2 * t, 2), SLOTS : 2 * SLOTS, :].reshape(2 * SLOTS, DIM)
-        s = dot_nt(keys, q) * SCALE2
-        d = dot_nt(values, g)
-        mp_ = jnp.max(s, axis=0, keepdims=True)
-        e = jnp.exp2(s - mp_)
-        lp = jnp.sum(e, axis=0, keepdims=True)
-        ip = jnp.sum(e * d, axis=0, keepdims=True)
-        stats = jnp.where(left, str_[2 * t], str_[2 * t + 1])
-        mo, lo, io, w = stats[0:1], stats[1:2], stats[2:3], stats[3:4]
-        m = jnp.maximum(mp_, mo)
-        fp = jnp.exp2(mp_ - m)
-        fo = jnp.exp2(mo - m)
-        inv = 1.0 / (lp * fp + lo * fo)
-        inner = (ip * fp + io * fo) * inv
-        coef = fp * inv * w
-        cols = pl.ds(pl.multiple_of(t * 128, 128), 128)
-        p = (e * coef).astype(BF16)
-        dsc = (e * (d - inner) * (coef * SCALE)).astype(BF16)
-        pw[:, :, cols] = p.reshape(4, 128, 128)
-        ds[:, :, cols] = dsc.reshape(4, 128, 128)
-        final = jnp.concatenate([m, inv, inner, jnp.zeros((5, DIM), F32)], axis=0)
-        fs[2 * t] = final
-        fs[2 * t + 1] = final
-        return 0
-
-    lax.fori_loop(0, 8, pair, 0, unroll=2)
-
-    q_all = xbr[:, 0:SLOTS, :].reshape(16 * SLOTS, DIM)
-    g_all = xbr[:, SLOTS : 2 * SLOTS, :].reshape(16 * SLOTS, DIM)
-    for b in y_others + [y]:
-        grad_k = dot_nn(ds[b], q_all)
-        grad_v = dot_nn(pw[b], g_all)
-        if b is not y:
-            sb1[b, 0] = grad_k.astype(BF16)
-            sb1[b, 1] = grad_v.astype(BF16)
-            remote(RS1, sb1.at[b], r1.at[y], y_peer(b)).start()
+    stats = jnp.concatenate(
+        [jnp.where(left, str_[2 * t], str_[2 * t + 1]) for t in range(8)], axis=1
+    )
+    m = stats[0:1]
+    for b in range(4):
+        m = jnp.maximum(m, part[b, 0:1, :])
+    fo = jnp.exp2(stats[0:1] - m)
+    total = stats[1:2] * fo
+    inner = stats[2:3] * (fo * SCALE)
+    for b in range(4):
+        f = jnp.exp2(part[b, 0:1, :] - m)
+        total = total + part[b, 1:2, :] * f
+        inner = inner + part[b, 2:3, :] * f
+        part[b, 3:4, :] = f
+    inv = 1.0 / total
+    inner = inner * inv
+    weights = inv * stats[3:4]
+
+    def finish(b):
+        coef = part[b, 3:4, :] * weights
+        for n in range(4):
+            cols = slice(n * 256, (n + 1) * 256)
+            p = exps[b, :, cols] * coef[:, cols]
+            pw[b, :, cols] = p.astype(BF16)
+            ds[b, :, cols] = (p * (prods[b, :, cols] - inner[:, cols])).astype(BF16)
+
+    q_all = xqr[...].reshape(16 * SLOTS, DIM)
+    g_all = xgr[...].reshape(16 * SLOTS, DIM)
+    for b in far_first:
+        finish(b)
+        sbv[b] = dot_nn(pw[b], g_all).astype(BF16)
+        remote(YSUM_V, sbv.at[b], rv.at[y], y_peer(b)).start()
+    for b in far_first:
+        sbk[b] = dot_nn(ds[b], q_all).astype(BF16)
+        remote(YSUM_K, sbk.at[b], rk.at[y], y_peer(b)).start()
+    finish(y)
+    final = jnp.concatenate(
+        [m, inv, inner * (1.0 / SCALE), jnp.zeros((5, 16 * SLOTS), F32)], axis=0
+    )
+    for t in range(8):
+        fs[2 * t] = final[:, t * DIM : (t + 1) * DIM]
+        fs[2 * t + 1] = final[:, t * DIM : (t + 1) * DIM]
+    keys = kb[...].reshape(PROMPT, DIM)
+    grad_v = dot_nn(pw[y], g_all)
+    grad_k = dot_nn(ds[y], q_all)
     for b in a_others:
         remote(FIN, fs.at[b], fr.at[a], a_peer(b)).start()
     fr[a] = fs[a]
@@ -244,17 +297,17 @@
         remote(DQ, dqs.at[b], dqr.at[a], a_peer(b)).start()
     dqr[a] = dqs[a]
 
-    arrived(RS1, r1.at[pl.ds(0, 3)])
-    for b in y_others:
-        grad_k = grad_k + r1[b, 0].astype(F32)
-        grad_v = grad_v + r1[b, 1].astype(F32)
-    for b in range(4):
-        sum1[b, 0] = grad_k[b * 32 : (b + 1) * 32]
-        sum1[b, 1] = grad_v[b * 32 : (b + 1) * 32]
-        sb2[b, 0] = grad_k[b * 32 : (b + 1) * 32].astype(BF16)
-        sb2[b, 1] = grad_v[b * 32 : (b + 1) * 32].astype(BF16)
-    for b in z_others:
-        remote(RS2, sb2.at[b], r2.at[z_hi], z_peer(b)).start()
+    def next_sum(total, kind_y, received, held, send, kind_z, target):
+        arrived(kind_y, received.at[pl.ds(0, 3)])
+        for b in y_others:
+            total = total + received[b].astype(F32)
+        held[...] = total.reshape(4, 32, DIM)
+        send[...] = total.astype(BF16).reshape(4, 32, DIM)
+        for b in z_others:
+            remote(kind_z, send.at[b], target.at[z_hi], z_peer(b)).start()
+
+    next_sum(grad_v, YSUM_V, rv, hv, szv, ZSUM_V, rzv)
+    next_sum(grad_k, YSUM_K, rk, hk, szk, ZSUM_K, rzk)
 
     arrived(FIN, fr.at[pl.ds(0, 15)])
     arrived(DQ, dqr.at[pl.ds(0, 15)])
@@ -269,8 +322,8 @@
         e = own_e[h]
         p = (e * coef).astype(BF16)
         dsc = (e * (own_d[h] - inner) * (coef * SCALE)).astype(BF16)
-        dvo[:, cols] = dot_nn(p, jnp.concatenate([xb[h, SLOTS:, :], nothing], axis=0)).astype(BF16)
-        dko[:, cols] = dot_nn(dsc, jnp.concatenate([xb[h, :SLOTS, :], nothing], axis=0)).astype(BF16)
+        dvo[:, cols] = dot_nn(p, jnp.concatenate([xg[h], nothing], axis=0)).astype(BF16)
+        dko[:, cols] = dot_nn(dsc, jnp.concatenate([xq[h], nothing], axis=0)).astype(BF16)
         dqo[:, cols] = (dot_tn(dsc, ck[:, cols])[:SLOTS] + dqr[h].astype(F32)).astype(BF16)
     stores = [
         pltpu.make_async_copy(src, dst, out_sem.at[n])
@@ -281,20 +334,21 @@
     for store in stores[:3]:
         store.start()
 
-    arrived(RS2, r2.at[pl.ds(0, 3)])
+    arrived(ZSUM_V, rzv.at[pl.ds(0, 3)])
+    arrived(ZSUM_K, rzk.at[pl.ds(0, 3)])
     line = lax.broadcasted_iota(jnp.int32, (16, 8, DIM), 1)
     lines = jnp.zeros((16, 8, DIM), F32)
-    for kv in range(2):
-        part = sum1[z_hi, kv]
+    for kv, (held, received) in enumerate(((hk, rzk), (hv, rzv))):
+        part = held[z_hi]
         for b in z_others:
-            part = part + r2[b, kv].astype(F32)
+            part = part + received[b].astype(F32)
         for r in range(2):
             lines = jnp.where(line == kv * 2 + r, part[r * 16 : (r + 1) * 16][:, None, :], lines)
     t3[...] = lines
     for b in a_others:
-        remote(RS3, t3.at[b], r3.at[a], a_peer(b)).start()
+        remote(OUT, t3.at[b], r3.at[a], a_peer(b)).start()
     r3[a] = t3[a]
-    arrived(RS3, r3.at[pl.ds(0, 15)])
+    arrived(OUT, r3.at[pl.ds(0, 15)])
     for h in range(HEADS):
         cols = slice(h * DIM, (h + 1) * DIM)
         gko[:, cols] = r3[h, 0:2, :].astype(BF16)
@@ -304,16 +358,21 @@
         store.start()
 
     sent(KV, kvs.at[pl.ds(0, 15)])
-    sent(QG, xb.at[pl.ds(0, 15)])
-    sent(ZKV, kvb.at[0, pl.ds(0, 3)])
+    sent(QUERY, xq.at[pl.ds(0, 15)])
+    sent(GRAD, xg.at[pl.ds(0, 15)])
+    sent(ZK, kb.at[0, pl.ds(0, 3)])
+    sent(ZV, vb.at[0, pl.ds(0, 3)])
     sent(ZSUM, gsumr.at[pl.ds(0, 3)])
-    sent(YKV, kvb.at[pl.ds(0, 3)])
+    sent(YK, kb.at[pl.ds(0, 3)])
+    sent(YV, vb.at[pl.ds(0, 3)])
     sent(OWN, st.at[pl.ds(0, 15)])
     sent(FIN, fs.at[pl.ds(0, 15)])
     sent(DQ, dqs.at[pl.ds(0, 15)])
-    sent(RS1, sb1.at[pl.ds(0, 3)])
-    sent(RS2, sb2.at[pl.ds(0, 3)])
-    sent(RS3, t3.at[pl.ds(0, 15)])
+    sent(YSUM_V, sbv.at[pl.ds(0, 3)])
+    sent(YSUM_K, sbk.at[pl.ds(0, 3)])
+    sent(ZSUM_V, szv.at[pl.ds(0, 3)])
+    sent(ZSUM_K, szk.at[pl.ds(0, 3)])
+    sent(OUT, t3.at[pl.ds(0, 15)])
     for store in stores:
         store.wait()
 
@@ -366,11 +425,14 @@
             V((ROWS, WIDTH), BF16),
             V((ROWS, WIDTH), BF16),
             V((SLOTS, WIDTH), BF16),
-            V((16, 128, DIM), BF16),
-            V((16, 128, DIM), BF16),
-            V((16, 8, DIM), F32),
-            V((16, 8, DIM), F32),
-            V((4, 4, 2, 32, DIM), BF16),
+            V((16, SLOTS, DIM), BF16),
+            V((16, SLOTS, DIM), BF16),
+            V((16, SLOTS, DIM), BF16),
+            V((16, SLOTS, DIM), BF16),
+            V((16, 8, DIM), F32),
+            V((16, 8, DIM), F32),
+            V((4, 4, 32, DIM), BF16),
+            V((4, 4, 32, DIM), BF16),
             V((8, DIM), F32),
             V((4, 8, DIM), F32),
             V((16, 128, DIM), F32),
@@ -379,13 +441,21 @@
             V((16, 8, DIM), F32),
             V((16, 8, DIM), F32),
             V((16, 8, DIM), F32),
+            V((4, 128, 16 * SLOTS), F32),
+            V((4, 128, 16 * SLOTS), F32),
+            V((4, 8, 16 * SLOTS), F32),
             V((4, 128, 16 * SLOTS), BF16),
             V((4, 128, 16 * SLOTS), BF16),
-            V((4, 2, 128, DIM), BF16),
-            V((4, 2, 128, DIM), BF16),
-            V((4, 2, 32, DIM), F32),
-            V((4, 2, 32, DIM), BF16),
-            V((4, 2, 32, DIM), BF16),
+            V((4, 128, DIM), BF16),
+            V((4, 128, DIM), BF16),
+            V((4, 128, DIM), BF16),
+            V((4, 128, DIM), BF16),
+            V((4, 32, DIM), F32),
+            V((4, 32, DIM), F32),
+            V((4, 32, DIM), BF16),
+            V((4, 32, DIM), BF16),
+            V((4, 32, DIM), BF16),
+            V((4, 32, DIM), BF16),
             V((16, 8, DIM), F32),
             V((16, 8, DIM), F32),
             V((16, SLOTS, DIM), BF16),
@@ -399,6 +469,7 @@
             pltpu.SemaphoreType.DMA((5,)),
             pltpu.SemaphoreType.DMA((KINDS,)),
             pltpu.SemaphoreType.DMA((KINDS,)),
+            pltpu.SemaphoreType.DMA((2, 4)),
         ],
         compiler_params=pltpu.CompilerParams(
             collective_id=0, has_side_effects=True, vmem_limit_bytes=60 * 1024 * 1024

time: 47.3 us -> 45.5 us (0.962)
  Pallas kernels: 45.9 us -> 44 us
    pallas_call x1, Pallas kernels: 43.8 us -> 41.9 us  [shards(): pl.pallas_call(kernel, out_shape=(jax.ShapeDtypeStruct((SLOTS, WIDTH), BF...]
where the time goes in v3:
time: 45.5 us; the launch traced here: 45.3 us
  Pallas kernels  44 us (97%)
  between operations  1.29 us (3%)
    pallas_call x1, Pallas kernels, shards(): pl.pallas_call(kernel, out_shape=(jax.ShapeDtypeStruct((SLOTS, WIDTH), BF...  41.9 us
    pallas_call x1, Pallas kernels, shards(): pl.pallas_call(store_all, out_shape=[jax.ShapeDtypeStruct(grad.shape, BF1...  2.12 us

profile of v3, /device:TPU:1, one launch (start us, length us, event | category | flops | bytes accessed | tf_op | source)
XLA Modules:
  0.0 45.3 jit_solution(10715886080242574144)
XLA Ops:
  1.3 41.9 %shard_map.119 = (bf16[64,2048]{1,0:T(8,128)(2,1)}, bf16[128,2048]{1,0:T(8,128)(2,1)}, bf16[128,2048]{1,0:T(8,128)(2,1)}, bf16[2,2048]{1,0:T(2,128)(2,1)}, bf16[2,2048]{1,0:T(2,128)(2,1)}) custom-call(bf16[2,2048]{1,0:T(2,128)(2,1)} %pk_hbm.1, bf16[2,2048]{1,0:T(2,128)(2,1)} %pv_hbm.1, f32[1,1]{1,0:T(1,128)S(6)} %copy.13.rw_hbm, s32[1,64]{1,0:T(1,128)} %bitcast.12, ...), custom_call_target="tpu_custom_call" | custom-call | tf_op jit(solution)/shard_map/pallas_call | solution.py:408
  43.2 2.1 %shard_map.120 = (bf16[64,2048]{1,0:T(8,128)(2,1)}, bf16[128,2048]{1,0:T(8,128)(2,1)}, bf16[128,2048]{1,0:T(8,128)(2,1)}, bf16[2,2048]{1,0:T(2,128)(2,1)}, bf16[2,2048]{1,0:T(2,128)(2,1)}) custom-call(bf16[64,2048]{1,0:T(8,128)(2,1)} %get-tuple-element.15.refs_0_, bf16[128,2048]{1,0:T(8,128)(2,1)} %get-tuple-element.16.refs_1_, ...), custom_call_target="tpu_custom_call" | custom-call | tf_op jit(solution)/shard_map/pallas_call | solution.py:481

commit v4 on v3

--- a/solution.py
+++ b/solution.py
@@ -39,7 +39,7 @@
     dq_hbm, dk_hbm, dv_hbm, gk_hbm, gv_hbm,
     pk, pv, rw, mp, cq, ck, cv, go, xq, xqr, xg, xgr, kvs, kvr, kb, vb, gsum, gsumr, own_e, own_d, st, str_,
     fs, fr, exps, prods, part, pw, ds,
-    sbk, sbv, rk, rv, hk, hv, szk, szv, rzk, rzv, t3, r3, dqs, dqr, dqo, dko, dvo, gko, gvo,
+    sbk, sbv, rk, rv, hk, hv, szk, szv, rzk, rzv, t3, r3, dqs, dqr, own_q, dqo, dko, dvo, gko, gvo,
     in_sem, out_sem, ss, rs, ry,
 ):
     grp = lax.axis_index("grp")
@@ -310,7 +310,6 @@
     next_sum(grad_k, YSUM_K, rk, hk, szk, ZSUM_K, rzk)
 
     arrived(FIN, fr.at[pl.ds(0, 15)])
-    arrived(DQ, dqr.at[pl.ds(0, 15)])
     here = left == (lax.rem(a, 2) == 0)
     nothing = jnp.zeros((SLOTS, DIM), BF16)
     for h in range(HEADS):
@@ -324,14 +323,14 @@
         dsc = (e * (own_d[h] - inner) * (coef * SCALE)).astype(BF16)
         dvo[:, cols] = dot_nn(p, jnp.concatenate([xg[h], nothing], axis=0)).astype(BF16)
         dko[:, cols] = dot_nn(dsc, jnp.concatenate([xq[h], nothing], axis=0)).astype(BF16)
-        dqo[:, cols] = (dot_tn(dsc, ck[:, cols])[:SLOTS] + dqr[h].astype(F32)).astype(BF16)
+        own_q[h] = dot_tn(dsc, ck[:, cols])[:SLOTS]
     stores = [
         pltpu.make_async_copy(src, dst, out_sem.at[n])
         for n, (src, dst) in enumerate(
             ((dqo, dq_hbm), (dko, dk_hbm), (dvo, dv_hbm), (gko, gk_hbm), (gvo, gv_hbm))
         )
     ]
-    for store in stores[:3]:
+    for store in stores[1:3]:
         store.start()
 
     arrived(ZSUM_V, rzv.at[pl.ds(0, 3)])
@@ -348,6 +347,10 @@
     for b in a_others:
         remote(OUT, t3.at[b], r3.at[a], a_peer(b)).start()
     r3[a] = t3[a]
+    arrived(DQ, dqr.at[pl.ds(0, 15)])
+    for h in range(HEADS):
+        dqo[:, h * DIM : (h + 1) * DIM] = (own_q[h] + dqr[h].astype(F32)).astype(BF16)
+    stores[0].start()
     arrived(OUT, r3.at[pl.ds(0, 15)])
     for h in range(HEADS):
         cols = slice(h * DIM, (h + 1) * DIM)
@@ -382,7 +385,7 @@
     parts = []
     for n in range(5):
         rows = sources[n].shape[0]
-        step = min(rows, SLOTS)
+        step = min(rows, 32)
         for first in range(0, rows, step):
             parts.append((n, pl.ds(first, step)))
     loads = [
@@ -460,6 +463,7 @@
             V((16, 8, DIM), F32),
             V((16, SLOTS, DIM), BF16),
             V((16, SLOTS, DIM), BF16),
+            V((16, SLOTS, DIM), F32),
             V((SLOTS, WIDTH), BF16),
             V((ROWS, WIDTH), BF16),
             V((ROWS, WIDTH), BF16),
@@ -483,7 +487,7 @@
         out_shape=[jax.ShapeDtypeStruct(grad.shape, BF16) for grad in grads],
         in_specs=[hbm] * 5,
         out_specs=[hbm] * 5,
-        scratch_shapes=[V(grad.shape, BF16) for grad in grads] + [pltpu.SemaphoreType.DMA((2, 7))],
+        scratch_shapes=[V(grad.shape, BF16) for grad in grads] + [pltpu.SemaphoreType.DMA((2, 12))],
         compiler_params=pltpu.CompilerParams(vmem_limit_bytes=60 * 1024 * 1024),
     )(*grads)
     return dq[None, None], dk[None, None], dv[None, None], gk, gv

time: 45.5 us -> 45.6 us (level)
  no operation moved by 1% of the time
where the time goes in v4:
time: 45.6 us; the launch traced here: 45.4 us
  Pallas kernels  44.1 us (97%)
  between operations  1.29 us (3%)
    pallas_call x1, Pallas kernels, shards(): pl.pallas_call(kernel, out_shape=(jax.ShapeDtypeStruct((SLOTS, WIDTH), BF...  41.9 us
    pallas_call x1, Pallas kernels, shards(): pl.pallas_call(store_all, out_shape=[jax.ShapeDtypeStruct(grad.shape, BF1...  2.25 us

profile of v4, /device:TPU:1, one launch (start us, length us, event | category | flops | bytes accessed | tf_op | source)
XLA Modules:
  0.0 45.4 jit_solution(17948772519197151239)
XLA Ops:
  1.3 41.9 %shard_map.119 = (bf16[64,2048]{1,0:T(8,128)(2,1)}, bf16[128,2048]{1,0:T(8,128)(2,1)}, bf16[128,2048]{1,0:T(8,128)(2,1)}, bf16[2,2048]{1,0:T(2,128)(2,1)}, bf16[2,2048]{1,0:T(2,128)(2,1)}) custom-call(bf16[2,2048]{1,0:T(2,128)(2,1)} %pk_hbm.1, bf16[2,2048]{1,0:T(2,128)(2,1)} %pv_hbm.1, f32[1,1]{1,0:T(1,128)S(6)} %copy.13.rw_hbm, s32[1,64]{1,0:T(1,128)} %bitcast.12, ...), custom_call_target="tpu_custom_call" | custom-call | tf_op jit(solution)/shard_map/pallas_call | solution.py:411
  43.2 2.2 %shard_map.120 = (bf16[64,2048]{1,0:T(8,128)(2,1)}, bf16[128,2048]{1,0:T(8,128)(2,1)}, bf16[128,2048]{1,0:T(8,128)(2,1)}, bf16[2,2048]{1,0:T(2,128)(2,1)}, bf16[2,2048]{1,0:T(2,128)(2,1)}) custom-call(bf16[64,2048]{1,0:T(8,128)(2,1)} %get-tuple-element.15.refs_0_, bf16[128,2048]{1,0:T(8,128)(2,1)} %get-tuple-element.16.refs_1_, ...), custom_call_target="tpu_custom_call" | custom-call | tf_op jit(solution)/shard_map/pallas_call | solution.py:485

commit v5 on v4

--- a/solution.py
+++ b/solution.py
@@ -61,8 +61,9 @@
     def y_peer(b):
         return {"grp": x_lo * 4 + b, "ctx": ctx}
 
-    a_others = [z_lo * 8 + lax.rem(a + k, 8) for k in range(1, 8)]
-    a_others += [(1 - z_lo) * 8 + lax.rem(a + k, 8) for k in range(8)]
+    a_same_z = [z_lo * 8 + lax.rem(a + k, 8) for k in range(1, 8)]
+    a_other_z = [(1 - z_lo) * 8 + lax.rem(a + k, 8) for k in range(8)]
+    a_others = a_same_z + a_other_z
     z_others = [lax.rem(z_hi + k, 4) for k in range(1, 4)]
     y_others = [lax.rem(y + k, 4) for k in range(1, 4)]
 
@@ -136,12 +137,15 @@
     picked = dot_tn(pick, cq[...])[:SLOTS].astype(BF16)
     for h in range(HEADS):
         xq[h] = picked[:, h * DIM : (h + 1) * DIM]
-    for b in a_others:
+    for b in a_same_z:
         remote(QUERY, xq.at[b], xqr.at[a], a_peer(b)).start()
     xqr[a] = xq[a]
     loads[5].wait()
     for h in range(HEADS):
         xg[h] = go[:, h * DIM : (h + 1) * DIM]
+    for b in a_same_z:
+        remote(GRAD, xg.at[b], xgr.at[a], a_peer(b)).start()
+    xgr[a] = xg[a]
 
     arrived(KV, kvr.at[pl.ds(0, 15)])
     blocks = kvr[...]
@@ -159,9 +163,10 @@
     gsum[...] = jnp.concatenate([count16, reward16, jnp.zeros((6, DIM), F32)], axis=0)
     for b in z_others:
         remote(ZSUM, gsum, gsumr.at[z_hi], z_peer(b)).start()
-    for b in a_others:
+    for b in a_other_z:
+        remote(QUERY, xq.at[b], xqr.at[a], a_peer(b)).start()
+    for b in a_other_z:
         remote(GRAD, xg.at[b], xgr.at[a], a_peer(b)).start()
-    xgr[a] = xg[a]
 
     def own_scores(h):
         q = xq[h]
@@ -293,7 +298,7 @@
         grad_q = dot_tn(ds[:, :, t * 128 : (t + 1) * 128].reshape(PROMPT, 2 * SLOTS), keys)
         dqs[2 * t] = grad_q[:SLOTS].astype(BF16)
         dqs[2 * t + 1] = grad_q[SLOTS:].astype(BF16)
-    for b in a_others:
+    for b in a_other_z + a_same_z:
         remote(DQ, dqs.at[b], dqr.at[a], a_peer(b)).start()
     dqr[a] = dqs[a]
 
@@ -385,7 +390,7 @@
     parts = []
     for n in range(5):
         rows = sources[n].shape[0]
-        step = min(rows, 32)
+        step = min(rows, 64)
         for first in range(0, rows, step):
             parts.append((n, pl.ds(first, step)))
     loads = [

time: 45.6 us -> 45.2 us (level)
  no operation moved by 1% of the time
where the time goes in v5:
time: 45.2 us; the launch traced here: 45.1 us
  Pallas kernels  43.8 us (97%)
  between operations  1.29 us (3%)
    pallas_call x1, Pallas kernels, shards(): pl.pallas_call(kernel, out_shape=(jax.ShapeDtypeStruct((SLOTS, WIDTH), BF...  41.6 us
    pallas_call x1, Pallas kernels, shards(): pl.pallas_call(store_all, out_shape=[jax.ShapeDtypeStruct(grad.shape, BF1...  2.21 us

profile of v5, /device:TPU:1, one launch (start us, length us, event | category | flops | bytes accessed | tf_op | source)
XLA Modules:
  0.0 45.1 jit_solution(3039927104026958734)
XLA Ops:
  1.3 41.6 %shard_map.119 = (bf16[64,2048]{1,0:T(8,128)(2,1)}, bf16[128,2048]{1,0:T(8,128)(2,1)}, bf16[128,2048]{1,0:T(8,128)(2,1)}, bf16[2,2048]{1,0:T(2,128)(2,1)}, bf16[2,2048]{1,0:T(2,128)(2,1)}) custom-call(bf16[2,2048]{1,0:T(2,128)(2,1)} %pk_hbm.1, bf16[2,2048]{1,0:T(2,128)(2,1)} %pv_hbm.1, f32[1,1]{1,0:T(1,128)S(6)} %copy.13.rw_hbm, s32[1,64]{1,0:T(1,128)} %bitcast.12, ...), custom_call_target="tpu_custom_call" | custom-call | tf_op jit(solution)/shard_map/pallas_call | solution.py:416
  42.9 2.2 %shard_map.120 = (bf16[64,2048]{1,0:T(8,128)(2,1)}, bf16[128,2048]{1,0:T(8,128)(2,1)}, bf16[128,2048]{1,0:T(8,128)(2,1)}, bf16[2,2048]{1,0:T(2,128)(2,1)}, bf16[2,2048]{1,0:T(2,128)(2,1)}) custom-call(bf16[64,2048]{1,0:T(8,128)(2,1)} %get-tuple-element.15.refs_0_, bf16[128,2048]{1,0:T(8,128)(2,1)} %get-tuple-element.16.refs_1_, ...), custom_call_target="tpu_custom_call" | custom-call | tf_op jit(solution)/shard_map/pallas_call | solution.py:490

commit v6 on v4

--- a/solution.py
+++ b/solution.py
@@ -136,9 +136,6 @@
     picked = dot_tn(pick, cq[...])[:SLOTS].astype(BF16)
     for h in range(HEADS):
         xq[h] = picked[:, h * DIM : (h + 1) * DIM]
-    for b in a_others:
-        remote(QUERY, xq.at[b], xqr.at[a], a_peer(b)).start()
-    xqr[a] = xq[a]
     loads[5].wait()
     for h in range(HEADS):
         xg[h] = go[:, h * DIM : (h + 1) * DIM]
@@ -160,8 +157,8 @@
     for b in z_others:
         remote(ZSUM, gsum, gsumr.at[z_hi], z_peer(b)).start()
     for b in a_others:
-        remote(GRAD, xg.at[b], xgr.at[a], a_peer(b)).start()
-    xgr[a] = xg[a]
+        remote(QUERY, xq.at[b], xqr.at[a], a_peer(b)).start()
+    xqr[a] = xq[a]
 
     def own_scores(h):
         q = xq[h]
@@ -184,7 +181,7 @@
 
     loads[6].wait()
     loads[7].wait()
-    for h in range(4):
+    for h in range(2):
         own_scores(h)
 
     arrived(ZK, kb.at[0, pl.ds(0, 3)])
@@ -193,7 +190,10 @@
     arrived(ZV, vb.at[0, pl.ds(0, 3)])
     for b in y_others:
         along_y(1, vb, y, b).start()
-    for h in range(4, HEADS):
+    for b in a_others:
+        remote(GRAD, xg.at[b], xgr.at[a], a_peer(b)).start()
+    xgr[a] = xg[a]
+    for h in range(2, HEADS):
         own_scores(h)
     arrived(ZSUM, gsumr.at[pl.ds(0, 3)])
     total = gsum[...]
@@ -293,9 +293,6 @@
         grad_q = dot_tn(ds[:, :, t * 128 : (t + 1) * 128].reshape(PROMPT, 2 * SLOTS), keys)
         dqs[2 * t] = grad_q[:SLOTS].astype(BF16)
         dqs[2 * t + 1] = grad_q[SLOTS:].astype(BF16)
-    for b in a_others:
-        remote(DQ, dqs.at[b], dqr.at[a], a_peer(b)).start()
-    dqr[a] = dqs[a]
 
     def next_sum(total, kind_y, received, held, send, kind_z, target):
         arrived(kind_y, received.at[pl.ds(0, 3)])
@@ -308,6 +305,9 @@
 
     next_sum(grad_v, YSUM_V, rv, hv, szv, ZSUM_V, rzv)
     next_sum(grad_k, YSUM_K, rk, hk, szk, ZSUM_K, rzk)
+    for b in a_others:
+        remote(DQ, dqs.at[b], dqr.at[a], a_peer(b)).start()
+    dqr[a] = dqs[a]
 
     arrived(FIN, fr.at[pl.ds(0, 15)])
     here = left == (lax.rem(a, 2) == 0)
@@ -385,7 +385,7 @@
     parts = []
     for n in range(5):
         rows = sources[n].shape[0]
-        step = min(rows, 32)
+        step = min(rows, 64)
         for first in range(0, rows, step):
             parts.append((n, pl.ds(first, step)))
     loads = [

time: 45.6 us -> 46.5 us (1.020)
  Pallas kernels: 44.1 us -> 45 us
    pallas_call x1, Pallas kernels: 41.9 us -> 42.8 us  [shards(): pl.pallas_call(kernel, out_shape=(jax.ShapeDtypeStruct((SLOTS, WIDTH), BF...]
where the time goes in v6:
time: 46.5 us; the launch traced here: 46.3 us
  Pallas kernels  45 us (97%)
  between operations  1.29 us (3%)
    pallas_call x1, Pallas kernels, shards(): pl.pallas_call(kernel, out_shape=(jax.ShapeDtypeStruct((SLOTS, WIDTH), BF...  42.8 us
    pallas_call x1, Pallas kernels, shards(): pl.pallas_call(store_all, out_shape=[jax.ShapeDtypeStruct(grad.shape, BF1...  2.21 us

profile of v6, /device:TPU:1, one launch (start us, length us, event | category | flops | bytes accessed | tf_op | source)
XLA Modules:
  0.0 46.3 jit_solution(9771617191603990353)
XLA Ops:
  1.3 42.8 %shard_map.119 = (bf16[64,2048]{1,0:T(8,128)(2,1)}, bf16[128,2048]{1,0:T(8,128)(2,1)}, bf16[128,2048]{1,0:T(8,128)(2,1)}, bf16[2,2048]{1,0:T(2,128)(2,1)}, bf16[2,2048]{1,0:T(2,128)(2,1)}) custom-call(bf16[2,2048]{1,0:T(2,128)(2,1)} %pk_hbm.1, bf16[2,2048]{1,0:T(2,128)(2,1)} %pv_hbm.1, f32[1,1]{1,0:T(1,128)S(6)} %copy.13.rw_hbm, s32[1,64]{1,0:T(1,128)} %bitcast.12, ...), custom_call_target="tpu_custom_call" | custom-call | tf_op jit(solution)/shard_map/pallas_call | solution.py:411
  44.1 2.2 %shard_map.120 = (bf16[64,2048]{1,0:T(8,128)(2,1)}, bf16[128,2048]{1,0:T(8,128)(2,1)}, bf16[128,2048]{1,0:T(8,128)(2,1)}, bf16[2,2048]{1,0:T(2,128)(2,1)}, bf16[2,2048]{1,0:T(2,128)(2,1)}) custom-call(bf16[64,2048]{1,0:T(8,128)(2,1)} %get-tuple-element.15.refs_0_, bf16[128,2048]{1,0:T(8,128)(2,1)} %get-tuple-element.16.refs_1_, ...), custom_call_target="tpu_custom_call" | custom-call | tf_op jit(solution)/shard_map/pallas_call | solution.py:485

commit v7 on v4

--- a/solution.py
+++ b/solution.py
@@ -163,16 +163,26 @@
         remote(GRAD, xg.at[b], xgr.at[a], a_peer(b)).start()
     xgr[a] = xg[a]
 
-    def own_scores(h):
-        q = xq[h]
-        g = xg[h]
-        s = dot_nt(ck[:, h * DIM : (h + 1) * DIM], jnp.concatenate([q, q], axis=0)) * SCALE2
-        d = dot_nt(cv[:, h * DIM : (h + 1) * DIM], jnp.concatenate([g, g], axis=0))
+    nothing = jnp.zeros((SLOTS, DIM), BF16)
+
+    def both(ref, t):
+        return jnp.concatenate(
+            [
+                jnp.concatenate([ref[2 * t], nothing], axis=1),
+                jnp.concatenate([nothing, ref[2 * t + 1]], axis=1),
+            ],
+            axis=0,
+        )
+
+    def own_scores(t):
+        cols = slice(t * 256, (t + 1) * 256)
+        s = dot_nt(ck[:, cols], both(xq, t)) * SCALE2
+        d = dot_nt(cv[:, cols], both(xg, t))
         m = jnp.max(s, axis=0, keepdims=True)
         e = jnp.exp2(s - m)
-        own_e[h] = e
-        own_d[h] = d
-        st[h] = jnp.concatenate(
+        own_e[t] = e
+        own_d[t] = d
+        st[t] = jnp.concatenate(
             [
                 m,
                 jnp.sum(e, axis=0, keepdims=True),
@@ -182,10 +192,18 @@
             axis=0,
         )
 
+    left = lax.broadcasted_iota(jnp.int32, (8, DIM), 1) < SLOTS
+    odd = jnp.broadcast_to(lax.rem(a, 2), (8, DIM)) == 1
+
+    def side_by_side(ref, t):
+        one, two = ref[2 * t], ref[2 * t + 1]
+        moved = pltpu.roll(jnp.where(odd, one, two), SLOTS, 1)
+        return jnp.where(left != odd, jnp.where(left, one, two), moved)
+
     loads[6].wait()
     loads[7].wait()
-    for h in range(4):
-        own_scores(h)
+    for t in range(2):
+        own_scores(t)
 
     arrived(ZK, kb.at[0, pl.ds(0, 3)])
     for b in y_others:
@@ -193,19 +211,19 @@
     arrived(ZV, vb.at[0, pl.ds(0, 3)])
     for b in y_others:
         along_y(1, vb, y, b).start()
-    for h in range(4, HEADS):
-        own_scores(h)
+    for t in range(2, 8):
+        own_scores(t)
     arrived(ZSUM, gsumr.at[pl.ds(0, 3)])
     total = gsum[...]
     for b in z_others:
         total = total + gsumr[b]
     weight = (reward - total[1:2] / 32.0) * (SLOTS * 32) / total[0:1]
     weight = jnp.where(pos2 < ROWS, weight, 0.0)
-    for h in range(HEADS):
-        st[h, 3:4, :] = weight
-    for b in a_others:
-        remote(OWN, st.at[b], str_.at[a], a_peer(b)).start()
-    str_[a] = st[a]
+    for t in range(8):
+        st[t, 3:4, :] = weight
+    for b in a_others:
+        remote(OWN, st.at[lax.div(b, 2)], str_.at[a], a_peer(b)).start()
+    str_[a] = st[lax.div(a, 2)]
 
     def key_block(b):
         block = kb[b].reshape(128, DIM)
@@ -240,10 +258,7 @@
         value_block(b)
 
     arrived(OWN, str_.at[pl.ds(0, 15)])
-    left = lax.broadcasted_iota(jnp.int32, (8, DIM), 1) < SLOTS
-    stats = jnp.concatenate(
-        [jnp.where(left, str_[2 * t], str_[2 * t + 1]) for t in range(8)], axis=1
-    )
+    stats = jnp.concatenate([side_by_side(str_, t) for t in range(8)], axis=1)
     m = stats[0:1]
     for b in range(4):
         m = jnp.maximum(m, part[b, 0:1, :])
@@ -281,14 +296,13 @@
         [m, inv, inner * (1.0 / SCALE), jnp.zeros((5, 16 * SLOTS), F32)], axis=0
     )
     for t in range(8):
-        fs[2 * t] = final[:, t * DIM : (t + 1) * DIM]
-        fs[2 * t + 1] = final[:, t * DIM : (t + 1) * DIM]
+        fs[t] = final[:, t * DIM : (t + 1) * DIM]
     keys = kb[...].reshape(PROMPT, DIM)
     grad_v = dot_nn(pw[y], g_all)
     grad_k = dot_nn(ds[y], q_all)
     for b in a_others:
-        remote(FIN, fs.at[b], fr.at[a], a_peer(b)).start()
-    fr[a] = fs[a]
+        remote(FIN, fs.at[lax.div(b, 2)], fr.at[a], a_peer(b)).start()
+    fr[a] = fs[lax.div(a, 2)]
     for t in range(8):
         grad_q = dot_tn(ds[:, :, t * 128 : (t + 1) * 128].reshape(PROMPT, 2 * SLOTS), keys)
         dqs[2 * t] = grad_q[:SLOTS].astype(BF16)
@@ -310,20 +324,19 @@
     next_sum(grad_k, YSUM_K, rk, hk, szk, ZSUM_K, rzk)
 
     arrived(FIN, fr.at[pl.ds(0, 15)])
-    here = left == (lax.rem(a, 2) == 0)
-    nothing = jnp.zeros((SLOTS, DIM), BF16)
-    for h in range(HEADS):
-        cols = slice(h * DIM, (h + 1) * DIM)
-        fin = fr[h]
-        fin = jnp.where(here, fin, jnp.concatenate([fin[:, SLOTS:], fin[:, :SLOTS]], axis=1))
+    for t in range(8):
+        cols = slice(t * 256, (t + 1) * 256)
+        fin = side_by_side(fr, t)
         m, inv, inner = fin[0:1], fin[1:2], fin[2:3]
-        coef = jnp.exp2(st[h, 0:1, :] - m) * inv * weight
-        e = own_e[h]
+        coef = jnp.exp2(st[t, 0:1, :] - m) * inv * weight
+        e = own_e[t]
         p = (e * coef).astype(BF16)
-        dsc = (e * (own_d[h] - inner) * (coef * SCALE)).astype(BF16)
-        dvo[:, cols] = dot_nn(p, jnp.concatenate([xg[h], nothing], axis=0)).astype(BF16)
-        dko[:, cols] = dot_nn(dsc, jnp.concatenate([xq[h], nothing], axis=0)).astype(BF16)
-        own_q[h] = dot_tn(dsc, ck[:, cols])[:SLOTS]
+        dsc = (e * (own_d[t] - inner) * (coef * SCALE)).astype(BF16)
+        dvo[:, cols] = dot_nn(p, both(xg, t)).astype(BF16)
+        dko[:, cols] = dot_nn(dsc, both(xq, t)).astype(BF16)
+        grad_q = dot_tn(dsc, ck[:, cols])
+        own_q[2 * t] = grad_q[:SLOTS, :DIM]
+        own_q[2 * t + 1] = grad_q[SLOTS:, DIM:]
     stores = [
         pltpu.make_async_copy(src, dst, out_sem.at[n])
         for n, (src, dst) in enumerate(
@@ -368,8 +381,8 @@
     sent(ZSUM, gsumr.at[pl.ds(0, 3)])
     sent(YK, kb.at[pl.ds(0, 3)])
     sent(YV, vb.at[pl.ds(0, 3)])
-    sent(OWN, st.at[pl.ds(0, 15)])
-    sent(FIN, fs.at[pl.ds(0, 15)])
+    sent(OWN, str_.at[pl.ds(0, 15)])
+    sent(FIN, fr.at[pl.ds(0, 15)])
     sent(DQ, dqs.at[pl.ds(0, 15)])
     sent(YSUM_V, sbv.at[pl.ds(0, 3)])
     sent(YSUM_K, sbk.at[pl.ds(0, 3)])
@@ -385,7 +398,7 @@
     parts = []
     for n in range(5):
         rows = sources[n].shape[0]
-        step = min(rows, 32)
+        step = min(rows, 64)
         for first in range(0, rows, step):
             parts.append((n, pl.ds(first, step)))
     loads = [
@@ -438,11 +451,11 @@
             V((4, 4, 32, DIM), BF16),
             V((8, DIM), F32),
             V((4, 8, DIM), F32),
-            V((16, 128, DIM), F32),
-            V((16, 128, DIM), F32),
+            V((8, 128, DIM), F32),
+            V((8, 128, DIM), F32),
+            V((8, 8, DIM), F32),
             V((16, 8, DIM), F32),
-            V((16, 8, DIM), F32),
-            V((16, 8, DIM), F32),
+            V((8, 8, DIM), F32),
             V((16, 8, DIM), F32),
             V((4, 128, 16 * SLOTS), F32),
             V((4, 128, 16 * SLOTS), F32),

time: 45.6 us -> 45.3 us (level)
  no operation moved by 1% of the time
where the time goes in v7:
time: 45.3 us; the launch traced here: 45.2 us
  Pallas kernels  43.9 us (97%)
  between operations  1.29 us (3%)
    pallas_call x1, Pallas kernels, shards(): pl.pallas_call(kernel, out_shape=(jax.ShapeDtypeStruct((SLOTS, WIDTH), BF...  41.7 us
    pallas_call x1, Pallas kernels, shards(): pl.pallas_call(store_all, out_shape=[jax.ShapeDtypeStruct(grad.shape, BF1...  2.21 us

profile of v7, /device:TPU:1, one launch (start us, length us, event | category | flops | bytes accessed | tf_op | source)
XLA Modules:
  0.0 45.2 jit_solution(11853541042634697048)
XLA Ops:
  1.3 41.7 %shard_map.119 = (bf16[64,2048]{1,0:T(8,128)(2,1)}, bf16[128,2048]{1,0:T(8,128)(2,1)}, bf16[128,2048]{1,0:T(8,128)(2,1)}, bf16[2,2048]{1,0:T(2,128)(2,1)}, bf16[2,2048]{1,0:T(2,128)(2,1)}) custom-call(bf16[2,2048]{1,0:T(2,128)(2,1)} %pk_hbm.1, bf16[2,2048]{1,0:T(2,128)(2,1)} %pv_hbm.1, f32[1,1]{1,0:T(1,128)S(6)} %copy.13.rw_hbm, s32[1,64]{1,0:T(1,128)} %bitcast.12, ...), custom_call_target="tpu_custom_call" | custom-call | tf_op jit(solution)/shard_map/pallas_call | solution.py:424
  43.0 2.2 %shard_map.120 = (bf16[64,2048]{1,0:T(8,128)(2,1)}, bf16[128,2048]{1,0:T(8,128)(2,1)}, bf16[128,2048]{1,0:T(8,128)(2,1)}, bf16[2,2048]{1,0:T(2,128)(2,1)}, bf16[2,2048]{1,0:T(2,128)(2,1)}) custom-call(bf16[64,2048]{1,0:T(8,128)(2,1)} %get-tuple-element.15.refs_0_, bf16[128,2048]{1,0:T(8,128)(2,1)} %get-tuple-element.16.refs_1_, ...), custom_call_target="tpu_custom_call" | custom-call | tf_op jit(solution)/shard_map/pallas_call | solution.py:498

commit v8 on v7

--- a/solution.py
+++ b/solution.py
@@ -36,10 +36,10 @@
 
 def kernel(
     pk_hbm, pv_hbm, rw_hbm, mp_hbm, cq_hbm, ck_hbm, cv_hbm, go_hbm,
-    dq_hbm, dk_hbm, dv_hbm, gk_hbm, gv_hbm,
+    dq_hbm, dk_hbm, dv_hbm, gp_hbm,
     pk, pv, rw, mp, cq, ck, cv, go, xq, xqr, xg, xgr, kvs, kvr, kb, vb, gsum, gsumr, own_e, own_d, st, str_,
     fs, fr, exps, prods, part, pw, ds,
-    sbk, sbv, rk, rv, hk, hv, szk, szv, rzk, rzv, t3, r3, dqs, dqr, own_q, dqo, dko, dvo, gko, gvo,
+    sbk, sbv, rk, rv, hk, hv, szk, szv, rzk, rzv, t3, dqs, dqr, own_q, dqo, dko, dvo,
     in_sem, out_sem, ss, rs, ry,
 ):
     grp = lax.axis_index("grp")
@@ -143,26 +143,6 @@
     for h in range(HEADS):
         xg[h] = go[:, h * DIM : (h + 1) * DIM]
 
-    arrived(KV, kvr.at[pl.ds(0, 15)])
-    blocks = kvr[...]
-    kb[y, z_hi, 0:16, :] = blocks[:, 0, :].astype(BF16)
-    kb[y, z_hi, 16:32, :] = blocks[:, 1, :].astype(BF16)
-    for b in z_others:
-        remote(ZK, kb.at[y, z_hi], kb.at[y, z_hi], z_peer(b)).start()
-    vb[y, z_hi, 0:16, :] = blocks[:, 2, :].astype(BF16)
-    vb[y, z_hi, 16:32, :] = blocks[:, 3, :].astype(BF16)
-    for b in z_others:
-        remote(ZV, vb.at[y, z_hi], vb.at[y, z_hi], z_peer(b)).start()
-    mine = lax.broadcasted_iota(jnp.int32, (16, DIM), 0) // 4 % 2 == x_lo
-    count16 = jnp.sum(jnp.where(mine, blocks[:, 4, :], 0.0), axis=0, keepdims=True)
-    reward16 = jnp.sum(jnp.where(mine, blocks[:, 5, :], 0.0), axis=0, keepdims=True)
-    gsum[...] = jnp.concatenate([count16, reward16, jnp.zeros((6, DIM), F32)], axis=0)
-    for b in z_others:
-        remote(ZSUM, gsum, gsumr.at[z_hi], z_peer(b)).start()
-    for b in a_others:
-        remote(GRAD, xg.at[b], xgr.at[a], a_peer(b)).start()
-    xgr[a] = xg[a]
-
     nothing = jnp.zeros((SLOTS, DIM), BF16)
 
     def both(ref, t):
@@ -202,7 +182,30 @@
 
     loads[6].wait()
     loads[7].wait()
-    for t in range(2):
+    for t in range(4):
+        own_scores(t)
+
+    arrived(KV, kvr.at[pl.ds(0, 15)])
+    blocks = kvr[...]
+    kb[y, z_hi, 0:16, :] = blocks[:, 0, :].astype(BF16)
+    kb[y, z_hi, 16:32, :] = blocks[:, 1, :].astype(BF16)
+    for b in z_others:
+        remote(ZK, kb.at[y, z_hi], kb.at[y, z_hi], z_peer(b)).start()
+    vb[y, z_hi, 0:16, :] = blocks[:, 2, :].astype(BF16)
+    vb[y, z_hi, 16:32, :] = blocks[:, 3, :].astype(BF16)
+    for b in z_others:
+        remote(ZV, vb.at[y, z_hi], vb.at[y, z_hi], z_peer(b)).start()
+    mine = lax.broadcasted_iota(jnp.int32, (16, DIM), 0) // 4 % 2 == x_lo
+    count16 = jnp.sum(jnp.where(mine, blocks[:, 4, :], 0.0), axis=0, keepdims=True)
+    reward16 = jnp.sum(jnp.where(mine, blocks[:, 5, :], 0.0), axis=0, keepdims=True)
+    gsum[...] = jnp.concatenate([count16, reward16, jnp.zeros((6, DIM), F32)], axis=0)
+    for b in z_others:
+        remote(ZSUM, gsum, gsumr.at[z_hi], z_peer(b)).start()
+    for b in a_others:
+        remote(GRAD, xg.at[b], xgr.at[a], a_peer(b)).start()
+    xgr[a] = xg[a]
+
+    for t in range(4, 8):
         own_scores(t)
 
     arrived(ZK, kb.at[0, pl.ds(0, 3)])
@@ -211,8 +214,6 @@
     arrived(ZV, vb.at[0, pl.ds(0, 3)])
     for b in y_others:
         along_y(1, vb, y, b).start()
-    for t in range(2, 8):
-        own_scores(t)
     arrived(ZSUM, gsumr.at[pl.ds(0, 3)])
     total = gsum[...]
     for b in z_others:
@@ -251,12 +252,6 @@
     for b in near_first:
         along_y(0, kb, b, b).wait_recv()
         key_block(b)
-    arrived(GRAD, xgr.at[pl.ds(0, 15)])
-    value_block(y)
-    for b in near_first:
-        along_y(1, vb, b, b).wait_recv()
-        value_block(b)
-
     arrived(OWN, str_.at[pl.ds(0, 15)])
     stats = jnp.concatenate([side_by_side(str_, t) for t in range(8)], axis=1)
     m = stats[0:1]
@@ -264,31 +259,46 @@
         m = jnp.maximum(m, part[b, 0:1, :])
     fo = jnp.exp2(stats[0:1] - m)
     total = stats[1:2] * fo
-    inner = stats[2:3] * (fo * SCALE)
     for b in range(4):
         f = jnp.exp2(part[b, 0:1, :] - m)
         total = total + part[b, 1:2, :] * f
-        inner = inner + part[b, 2:3, :] * f
         part[b, 3:4, :] = f
     inv = 1.0 / total
-    inner = inner * inv
-    weights = inv * stats[3:4]
-
-    def finish(b):
-        coef = part[b, 3:4, :] * weights
+    weights = stats[3:4]
+
+    def probabilities(b):
+        coef = part[b, 3:4, :] * inv
         for n in range(4):
             cols = slice(n * 256, (n + 1) * 256)
             p = exps[b, :, cols] * coef[:, cols]
-            pw[b, :, cols] = p.astype(BF16)
-            ds[b, :, cols] = (p * (prods[b, :, cols] - inner[:, cols])).astype(BF16)
-
+            exps[b, :, cols] = p
+            pw[b, :, cols] = (p * weights[:, cols]).astype(BF16)
+
+    arrived(GRAD, xgr.at[pl.ds(0, 15)])
     q_all = xqr[...].reshape(16 * SLOTS, DIM)
     g_all = xgr[...].reshape(16 * SLOTS, DIM)
     for b in far_first:
-        finish(b)
+        probabilities(b)
         sbv[b] = dot_nn(pw[b], g_all).astype(BF16)
         remote(YSUM_V, sbv.at[b], rv.at[y], y_peer(b)).start()
+    probabilities(y)
+
+    value_block(y)
+    for b in near_first:
+        along_y(1, vb, b, b).wait_recv()
+        value_block(b)
+    inner = stats[2:3] * (fo * inv * SCALE)
+    for b in range(4):
+        inner = inner + part[b, 2:3, :]
+
+    def finish(b):
+        for n in range(4):
+            cols = slice(n * 256, (n + 1) * 256)
+            dscore = exps[b, :, cols] * (prods[b, :, cols] - inner[:, cols])
+            ds[b, :, cols] = (dscore * weights[:, cols]).astype(BF16)
+
     for b in far_first:
+        finish(b)
         sbk[b] = dot_nn(ds[b], q_all).astype(BF16)
         remote(YSUM_K, sbk.at[b], rk.at[y], y_peer(b)).start()
     finish(y)
@@ -340,7 +350,7 @@
     stores = [
         pltpu.make_async_copy(src, dst, out_sem.at[n])
         for n, (src, dst) in enumerate(
-            ((dqo, dq_hbm), (dko, dk_hbm), (dvo, dv_hbm), (gko, gk_hbm), (gvo, gv_hbm))
+            ((dqo, dq_hbm), (dko, dk_hbm), (dvo, dv_hbm), (t3.at[a], gp_hbm.at[a]))
         )
     ]
     for store in stores[1:3]:
@@ -358,20 +368,13 @@
             lines = jnp.where(line == kv * 2 + r, part[r * 16 : (r + 1) * 16][:, None, :], lines)
     t3[...] = lines
     for b in a_others:
-        remote(OUT, t3.at[b], r3.at[a], a_peer(b)).start()
-    r3[a] = t3[a]
+        remote(OUT, t3.at[b], gp_hbm.at[a], a_peer(b)).start()
+    stores[3].start()
     arrived(DQ, dqr.at[pl.ds(0, 15)])
     for h in range(HEADS):
         dqo[:, h * DIM : (h + 1) * DIM] = (own_q[h] + dqr[h].astype(F32)).astype(BF16)
     stores[0].start()
-    arrived(OUT, r3.at[pl.ds(0, 15)])
-    for h in range(HEADS):
-        cols = slice(h * DIM, (h + 1) * DIM)
-        gko[:, cols] = r3[h, 0:2, :].astype(BF16)
-        gvo[:, cols] = r3[h, 2:4, :].astype(BF16)
-
-    for store in stores[3:]:
-        store.start()
+    arrived(OUT, gp_hbm.at[pl.ds(0, 15)])
 
     sent(KV, kvs.at[pl.ds(0, 15)])
     sent(QUERY, xq.at[pl.ds(0, 15)])
@@ -393,26 +396,29 @@
         store.wait()
 
 
-def store_all(*refs):
-    sources, targets, held, sem = refs[:5], refs[5:10], refs[10:15], refs[15]
-    parts = []
-    for n in range(5):
-        rows = sources[n].shape[0]
-        step = min(rows, 64)
-        for first in range(0, rows, step):
-            parts.append((n, pl.ds(first, step)))
-    loads = [
-        pltpu.make_async_copy(sources[n].at[span], held[n].at[span], sem.at[0, p])
-        for p, (n, span) in enumerate(parts)
-    ]
-    stores = [
-        pltpu.make_async_copy(held[n].at[span], targets[n].at[span], sem.at[1, p])
-        for p, (n, span) in enumerate(parts)
-    ]
-    for load in loads:
+def store_all(dq, dk, dv, gp, dq_out, dk_out, dv_out, gk_out, gv_out, *scratch):
+    dq_held, dk_held, dv_held, gp_held, gk_held, gv_held, in_sem, out_sem = scratch
+    parts = [(gp, gp_held)]
+    stores = []
+    for source, held, target in ((dq, dq_held, dq_out), (dk, dk_held, dk_out), (dv, dv_held, dv_out)):
+        for first in range(0, source.shape[0], SLOTS):
+            span = pl.ds(first, SLOTS)
+            parts.append((source.at[span], held.at[span]))
+            stores.append((held.at[span], target.at[span]))
+    stores += [(gk_held, gk_out), (gv_held, gv_out)]
+    loads = [pltpu.make_async_copy(*pair, in_sem.at[n]) for n, pair in enumerate(parts)]
+    stores = [pltpu.make_async_copy(*pair, out_sem.at[n]) for n, pair in enumerate(stores)]
+    for load in loads[1:] + loads[:1]:
         load.start()
-    for load, store in zip(loads, stores):
+    for load, store in zip(loads[1:], stores):
         load.wait()
+        store.start()
+    loads[0].wait()
+    for h in range(HEADS):
+        cols = slice(h * DIM, (h + 1) * DIM)
+        gk_held[:, cols] = gp_held[h, 0:2, :].astype(BF16)
+        gv_held[:, cols] = gp_held[h, 2:4, :].astype(BF16)
+    for store in stores[-2:]:
         store.start()
     for store in stores:
         store.wait()
@@ -427,11 +433,10 @@
             jax.ShapeDtypeStruct((SLOTS, WIDTH), BF16),
             jax.ShapeDtypeStruct((ROWS, WIDTH), BF16),
             jax.ShapeDtypeStruct((ROWS, WIDTH), BF16),
-            jax.ShapeDtypeStruct((2, WIDTH), BF16),
-            jax.ShapeDtypeStruct((2, WIDTH), BF16),
+            jax.ShapeDtypeStruct((16, 8, DIM), F32),
         ),
         in_specs=[hbm] * 8,
-        out_specs=(hbm,) * 5,
+        out_specs=(hbm,) * 4,
         scratch_shapes=[
             V((2, WIDTH), BF16),
             V((2, WIDTH), BF16),
@@ -473,17 +478,14 @@
             V((4, 32, DIM), BF16),
             V((4, 32, DIM), BF16),
             V((16, 8, DIM), F32),
-            V((16, 8, DIM), F32),
             V((16, SLOTS, DIM), BF16),
             V((16, SLOTS, DIM), BF16),
             V((16, SLOTS, DIM), F32),
             V((SLOTS, WIDTH), BF16),
             V((ROWS, WIDTH), BF16),
             V((ROWS, WIDTH), BF16),
-            V((2, WIDTH), BF16),
-            V((2, WIDTH), BF16),
             pltpu.SemaphoreType.DMA((8,)),
-            pltpu.SemaphoreType.DMA((5,)),
+            pltpu.SemaphoreType.DMA((4,)),
             pltpu.SemaphoreType.DMA((KINDS,)),
             pltpu.SemaphoreType.DMA((KINDS,)),
             pltpu.SemaphoreType.DMA((2, 4)),
@@ -495,12 +497,21 @@
         prompt_k, prompt_v, rewards, mask_pos[0], comp_q[0, 0], comp_k[0, 0], comp_v[0, 0],
         grad_out[0, 0],
     )
+    wide = [jax.ShapeDtypeStruct(grad.shape, BF16) for grad in grads[:3]]
+    thin = [jax.ShapeDtypeStruct((2, WIDTH), BF16)] * 2
     dq, dk, dv, gk, gv = pl.pallas_call(
         store_all,
-        out_shape=[jax.ShapeDtypeStruct(grad.shape, BF16) for grad in grads],
-        in_specs=[hbm] * 5,
+        out_shape=wide + thin,
+        in_specs=[hbm] * 4,
         out_specs=[hbm] * 5,
-        scratch_shapes=[V(grad.shape, BF16) for grad in grads] + [pltpu.SemaphoreType.DMA((2, 12))],
+        scratch_shapes=[V(grad.shape, BF16) for grad in grads[:3]]
+        + [
+            V((16, 8, DIM), F32),
+            V((2, WIDTH), BF16),
+            V((2, WIDTH), BF16),
+            pltpu.SemaphoreType.DMA((6,)),
+            pltpu.SemaphoreType.DMA((7,)),
+        ],
         compiler_params=pltpu.CompilerParams(vmem_limit_bytes=60 * 1024 * 1024),
     )(*grads)
     return dq[None, None], dk[None, None], dv[None, None], gk, gv

time: 45.3 us -> 44.9 us (level)
  Pallas kernels: 43.9 us -> 43.4 us
where the time goes in v8:
time: 44.9 us; the launch traced here: 44.7 us
  Pallas kernels  43.4 us (97%)
  between operations  1.29 us (3%)
    pallas_call x1, Pallas kernels, shards(): pl.pallas_call(kernel, out_shape=(jax.ShapeDtypeStruct((SLOTS, WIDTH), BF...  41.3 us
    pallas_call x1, Pallas kernels, shards(): pl.pallas_call(store_all, out_shape=wide + thin, in_specs=[hbm] * 4, out_...  2.12 us

profile of v8, /device:TPU:1, one launch (start us, length us, event | category | flops | bytes accessed | tf_op | source)
XLA Modules:
  0.0 44.7 jit_solution(17168081340046585237)
XLA Ops:
  1.3 41.3 %shard_map.119 = (bf16[64,2048]{1,0:T(8,128)(2,1)}, bf16[128,2048]{1,0:T(8,128)(2,1)}, bf16[128,2048]{1,0:T(8,128)(2,1)}, f32[16,8,128]{2,1,0:T(8,128)}) custom-call(bf16[2,2048]{1,0:T(2,128)(2,1)} %pk_hbm.1, bf16[2,2048]{1,0:T(2,128)(2,1)} %pv_hbm.1, f32[1,1]{1,0:T(1,128)S(6)} %copy.13.rw_hbm, s32[1,64]{1,0:T(1,128)} %bitcast.12, ...), custom_call_target="tpu_custom_call" | custom-call | tf_op jit(solution)/shard_map/pallas_call | solution.py:430
  42.6 2.1 %shard_map.120 = (bf16[64,2048]{1,0:T(8,128)(2,1)}, bf16[128,2048]{1,0:T(8,128)(2,1)}, bf16[128,2048]{1,0:T(8,128)(2,1)}, bf16[2,2048]{1,0:T(2,128)(2,1)}, bf16[2,2048]{1,0:T(2,128)(2,1)}) custom-call(bf16[64,2048]{1,0:T(8,128)(2,1)} %get-tuple-element.14.dq, bf16[128,2048]{1,0:T(8,128)(2,1)} %get-tuple-element.15.dk, ...), custom_call_target="tpu_custom_call" | custom-call | tf_op jit(solution)/shard_map/pallas_call | solution.py:502

commit v9 on v8

--- a/solution.py
+++ b/solution.py
@@ -136,9 +136,6 @@
     picked = dot_tn(pick, cq[...])[:SLOTS].astype(BF16)
     for h in range(HEADS):
         xq[h] = picked[:, h * DIM : (h + 1) * DIM]
-    for b in a_others:
-        remote(QUERY, xq.at[b], xqr.at[a], a_peer(b)).start()
-    xqr[a] = xq[a]
     loads[5].wait()
     for h in range(HEADS):
         xg[h] = go[:, h * DIM : (h + 1) * DIM]
@@ -201,6 +198,9 @@
     gsum[...] = jnp.concatenate([count16, reward16, jnp.zeros((6, DIM), F32)], axis=0)
     for b in z_others:
         remote(ZSUM, gsum, gsumr.at[z_hi], z_peer(b)).start()
+    for b in a_others:
+        remote(QUERY, xq.at[b], xqr.at[a], a_peer(b)).start()
+    xqr[a] = xq[a]
     for b in a_others:
         remote(GRAD, xg.at[b], xgr.at[a], a_peer(b)).start()
     xgr[a] = xg[a]

time: 44.9 us -> 45.3 us (level)
  Pallas kernels: 43.4 us -> 43.9 us
where the time goes in v9:
time: 45.3 us; the launch traced here: 45.2 us
  Pallas kernels  43.9 us (97%)
  between operations  1.29 us (3%)
    pallas_call x1, Pallas kernels, shards(): pl.pallas_call(kernel, out_shape=(jax.ShapeDtypeStruct((SLOTS, WIDTH), BF...  41.8 us
    pallas_call x1, Pallas kernels, shards(): pl.pallas_call(store_all, out_shape=wide + thin, in_specs=[hbm] * 4, out_...  2.12 us

profile of v9, /device:TPU:1, one launch (start us, length us, event | category | flops | bytes accessed | tf_op | source)
XLA Modules:
  0.0 45.2 jit_solution(9546182026489742114)
XLA Ops:
  1.3 41.8 %shard_map.119 = (bf16[64,2048]{1,0:T(8,128)(2,1)}, bf16[128,2048]{1,0:T(8,128)(2,1)}, bf16[128,2048]{1,0:T(8,128)(2,1)}, f32[16,8,128]{2,1,0:T(8,128)}) custom-call(bf16[2,2048]{1,0:T(2,128)(2,1)} %pk_hbm.1, bf16[2,2048]{1,0:T(2,128)(2,1)} %pv_hbm.1, f32[1,1]{1,0:T(1,128)S(6)} %copy.13.rw_hbm, s32[1,64]{1,0:T(1,128)} %bitcast.12, ...), custom_call_target="tpu_custom_call" | custom-call | tf_op jit(solution)/shard_map/pallas_call | solution.py:430
  43.0 2.1 %shard_map.120 = (bf16[64,2048]{1,0:T(8,128)(2,1)}, bf16[128,2048]{1,0:T(8,128)(2,1)}, bf16[128,2048]{1,0:T(8,128)(2,1)}, bf16[2,2048]{1,0:T(2,128)(2,1)}, bf16[2,2048]{1,0:T(2,128)(2,1)}) custom-call(bf16[64,2048]{1,0:T(8,128)(2,1)} %get-tuple-element.14.dq, bf16[128,2048]{1,0:T(8,128)(2,1)} %get-tuple-element.15.dk, ...), custom_call_target="tpu_custom_call" | custom-call | tf_op jit(solution)/shard_map/pallas_call | solution.py:502

commit v10 on v9

--- a/solution.py
+++ b/solution.py
@@ -38,7 +38,7 @@
     pk_hbm, pv_hbm, rw_hbm, mp_hbm, cq_hbm, ck_hbm, cv_hbm, go_hbm,
     dq_hbm, dk_hbm, dv_hbm, gp_hbm,
     pk, pv, rw, mp, cq, ck, cv, go, xq, xqr, xg, xgr, kvs, kvr, kb, vb, gsum, gsumr, own_e, own_d, st, str_,
-    fs, fr, exps, prods, part, pw, ds,
+    fs, fr, exps, prods, part, pw, ds, kt,
     sbk, sbv, rk, rv, hk, hv, szk, szv, rzk, rzv, t3, dqs, dqr, own_q, dqo, dko, dvo,
     in_sem, out_sem, ss, rs, ry,
 ):
@@ -282,6 +282,10 @@
         sbv[b] = dot_nn(pw[b], g_all).astype(BF16)
         remote(YSUM_V, sbv.at[b], rv.at[y], y_peer(b)).start()
     probabilities(y)
+    for b in range(4):
+        kt[:, b * 128 : (b + 1) * 128] = jnp.transpose(
+            kb[b].reshape(128, DIM).astype(F32)
+        ).astype(BF16)
 
     value_block(y)
     for b in near_first:
@@ -307,16 +311,18 @@
     )
     for t in range(8):
         fs[t] = final[:, t * DIM : (t + 1) * DIM]
-    keys = kb[...].reshape(PROMPT, DIM)
     grad_v = dot_nn(pw[y], g_all)
     grad_k = dot_nn(ds[y], q_all)
     for b in a_others:
         remote(FIN, fs.at[lax.div(b, 2)], fr.at[a], a_peer(b)).start()
     fr[a] = fs[lax.div(a, 2)]
-    for t in range(8):
-        grad_q = dot_tn(ds[:, :, t * 128 : (t + 1) * 128].reshape(PROMPT, 2 * SLOTS), keys)
-        dqs[2 * t] = grad_q[:SLOTS].astype(BF16)
-        dqs[2 * t + 1] = grad_q[SLOTS:].astype(BF16)
+    for t in range(4):
+        cols = slice(t * 256, (t + 1) * 256)
+        grad_q = dot_nn(kt[...], ds[:, :, cols].reshape(PROMPT, 256))
+        for u in range(2):
+            turned = jnp.transpose(grad_q[:, u * 128 : (u + 1) * 128]).astype(BF16)
+            dqs[4 * t + 2 * u] = turned[:SLOTS]
+            dqs[4 * t + 2 * u + 1] = turned[SLOTS:]
     for b in a_others:
         remote(DQ, dqs.at[b], dqr.at[a], a_peer(b)).start()
     dqr[a] = dqs[a]
@@ -467,6 +473,7 @@
             V((4, 8, 16 * SLOTS), F32),
             V((4, 128, 16 * SLOTS), BF16),
             V((4, 128, 16 * SLOTS), BF16),
+            V((DIM, PROMPT), BF16),
             V((4, 128, DIM), BF16),
             V((4, 128, DIM), BF16),
             V((4, 128, DIM), BF16),

time: 45.3 us -> 45 us (level)
  no operation moved by 1% of the time
where the time goes in v10:
time: 45 us; the launch traced here: 44.8 us
  Pallas kernels  43.5 us (97%)
  between operations  1.29 us (3%)
    pallas_call x1, Pallas kernels, shards(): pl.pallas_call(kernel, out_shape=(jax.ShapeDtypeStruct((SLOTS, WIDTH), BF...  41.4 us
    pallas_call x1, Pallas kernels, shards(): pl.pallas_call(store_all, out_shape=wide + thin, in_specs=[hbm] * 4, out_...  2.12 us

profile of v10, /device:TPU:1, one launch (start us, length us, event | category | flops | bytes accessed | tf_op | source)
XLA Modules:
  0.0 44.8 jit_solution(8348905922166642483)
XLA Ops:
  1.3 41.4 %shard_map.119 = (bf16[64,2048]{1,0:T(8,128)(2,1)}, bf16[128,2048]{1,0:T(8,128)(2,1)}, bf16[128,2048]{1,0:T(8,128)(2,1)}, f32[16,8,128]{2,1,0:T(8,128)}) custom-call(bf16[2,2048]{1,0:T(2,128)(2,1)} %pk_hbm.1, bf16[2,2048]{1,0:T(2,128)(2,1)} %pv_hbm.1, f32[1,1]{1,0:T(1,128)S(6)} %copy.13.rw_hbm, s32[1,64]{1,0:T(1,128)} %bitcast.12, ...), custom_call_target="tpu_custom_call" | custom-call | tf_op jit(solution)/shard_map/pallas_call | solution.py:436
  42.7 2.1 %shard_map.120 = (bf16[64,2048]{1,0:T(8,128)(2,1)}, bf16[128,2048]{1,0:T(8,128)(2,1)}, bf16[128,2048]{1,0:T(8,128)(2,1)}, bf16[2,2048]{1,0:T(2,128)(2,1)}, bf16[2,2048]{1,0:T(2,128)(2,1)}) custom-call(bf16[64,2048]{1,0:T(8,128)(2,1)} %get-tuple-element.14.dq, bf16[128,2048]{1,0:T(8,128)(2,1)} %get-tuple-element.15.dk, ...), custom_call_target="tpu_custom_call" | custom-call | tf_op jit(solution)/shard_map/pallas_call | solution.py:509

commit v11 on v9

--- a/solution.py
+++ b/solution.py
@@ -36,10 +36,10 @@
 
 def kernel(
     pk_hbm, pv_hbm, rw_hbm, mp_hbm, cq_hbm, ck_hbm, cv_hbm, go_hbm,
-    dq_hbm, dk_hbm, dv_hbm, gp_hbm,
+    own_hbm, dqr, dk_hbm, dv_hbm, gp_hbm,
     pk, pv, rw, mp, cq, ck, cv, go, xq, xqr, xg, xgr, kvs, kvr, kb, vb, gsum, gsumr, own_e, own_d, st, str_,
     fs, fr, exps, prods, part, pw, ds,
-    sbk, sbv, rk, rv, hk, hv, szk, szv, rzk, rzv, t3, dqs, dqr, own_q, dqo, dko, dvo,
+    sbk, sbv, rk, rv, hk, hv, szk, szv, rzk, rzv, t3, dqs, dqo, dko, dvo,
     in_sem, out_sem, ss, rs, ry,
 ):
     grp = lax.axis_index("grp")
@@ -61,8 +61,18 @@
     def y_peer(b):
         return {"grp": x_lo * 4 + b, "ctx": ctx}
 
-    a_others = [z_lo * 8 + lax.rem(a + k, 8) for k in range(1, 8)]
-    a_others += [(1 - z_lo) * 8 + lax.rem(a + k, 8) for k in range(8)]
+    flips = [(dz, 0, 1, dc) for dz in (1, 0) for dc in (1, 0)]
+    flips += [(dz, 1, dx, dc) for dz in (1, 0) for dx in (1, 0) for dc in (1, 0)]
+    flips += [(1, 0, 0, 1), (1, 0, 0, 0), (0, 0, 0, 1)]
+
+    def flipped(bit, flip):
+        return 1 - bit if flip else bit
+
+    x_hi, core = lax.div(low, 2), lax.rem(low, 2)
+    a_others = [
+        flipped(z_lo, dz) * 8 + flipped(x_lo, dl) * 4 + flipped(x_hi, dh) * 2 + flipped(core, dc)
+        for dz, dl, dh, dc in flips
+    ]
     z_others = [lax.rem(z_hi + k, 4) for k in range(1, 4)]
     y_others = [lax.rem(y + k, 4) for k in range(1, 4)]
 
@@ -319,7 +329,8 @@
         dqs[2 * t + 1] = grad_q[SLOTS:].astype(BF16)
     for b in a_others:
         remote(DQ, dqs.at[b], dqr.at[a], a_peer(b)).start()
-    dqr[a] = dqs[a]
+    own_part = pltpu.make_async_copy(dqs.at[a], dqr.at[a], out_sem.at[4])
+    own_part.start()
 
     def next_sum(total, kind_y, received, held, send, kind_z, target):
         arrived(kind_y, received.at[pl.ds(0, 3)])
@@ -345,15 +356,15 @@
         dvo[:, cols] = dot_nn(p, both(xg, t)).astype(BF16)
         dko[:, cols] = dot_nn(dsc, both(xq, t)).astype(BF16)
         grad_q = dot_tn(dsc, ck[:, cols])
-        own_q[2 * t] = grad_q[:SLOTS, :DIM]
-        own_q[2 * t + 1] = grad_q[SLOTS:, DIM:]
+        dqo[2 * t] = grad_q[:SLOTS, :DIM].astype(BF16)
+        dqo[2 * t + 1] = grad_q[SLOTS:, DIM:].astype(BF16)
     stores = [
         pltpu.make_async_copy(src, dst, out_sem.at[n])
         for n, (src, dst) in enumerate(
-            ((dqo, dq_hbm), (dko, dk_hbm), (dvo, dv_hbm), (t3.at[a], gp_hbm.at[a]))
+            ((dqo, own_hbm), (dko, dk_hbm), (dvo, dv_hbm), (t3.at[a], gp_hbm.at[a]))
         )
     ]
-    for store in stores[1:3]:
+    for store in stores[:3]:
         store.start()
 
     arrived(ZSUM_V, rzv.at[pl.ds(0, 3)])
@@ -371,9 +382,6 @@
         remote(OUT, t3.at[b], gp_hbm.at[a], a_peer(b)).start()
     stores[3].start()
     arrived(DQ, dqr.at[pl.ds(0, 15)])
-    for h in range(HEADS):
-        dqo[:, h * DIM : (h + 1) * DIM] = (own_q[h] + dqr[h].astype(F32)).astype(BF16)
-    stores[0].start()
     arrived(OUT, gp_hbm.at[pl.ds(0, 15)])
 
     sent(KV, kvs.at[pl.ds(0, 15)])
@@ -392,34 +400,44 @@
     sent(ZSUM_V, szv.at[pl.ds(0, 3)])
     sent(ZSUM_K, szk.at[pl.ds(0, 3)])
     sent(OUT, t3.at[pl.ds(0, 15)])
-    for store in stores:
+    for store in stores + [own_part]:
         store.wait()
 
 
-def store_all(dq, dk, dv, gp, dq_out, dk_out, dv_out, gk_out, gv_out, *scratch):
-    dq_held, dk_held, dv_held, gp_held, gk_held, gv_held, in_sem, out_sem = scratch
-    parts = [(gp, gp_held)]
+def store_all(own, other, dk, dv, gp, dq_out, dk_out, dv_out, gk_out, gv_out, *scratch):
+    (
+        own_held, other_held, dk_held, dv_held, gp_held, dq_held, gk_held, gv_held,
+        in_sem, out_sem,
+    ) = scratch
+    pairs = [(own, own_held), (other, other_held), (gp, gp_held)]
     stores = []
-    for source, held, target in ((dq, dq_held, dq_out), (dk, dk_held, dk_out), (dv, dv_held, dv_out)):
-        for first in range(0, source.shape[0], SLOTS):
+    for source, held, target in ((dk, dk_held, dk_out), (dv, dv_held, dv_out)):
+        for first in range(0, ROWS, SLOTS):
             span = pl.ds(first, SLOTS)
-            parts.append((source.at[span], held.at[span]))
+            pairs.append((source.at[span], held.at[span]))
             stores.append((held.at[span], target.at[span]))
-    stores += [(gk_held, gk_out), (gv_held, gv_out)]
-    loads = [pltpu.make_async_copy(*pair, in_sem.at[n]) for n, pair in enumerate(parts)]
+    stores += [(dq_held, dq_out), (gk_held, gk_out), (gv_held, gv_out)]
+    loads = [pltpu.make_async_copy(*pair, in_sem.at[n]) for n, pair in enumerate(pairs)]
     stores = [pltpu.make_async_copy(*pair, out_sem.at[n]) for n, pair in enumerate(stores)]
-    for load in loads[1:] + loads[:1]:
+    for load in loads:
         load.start()
-    for load, store in zip(loads[1:], stores):
-        load.wait()
-        store.start()
     loads[0].wait()
+    loads[1].wait()
+    for h in range(HEADS):
+        cols = slice(h * DIM, (h + 1) * DIM)
+        total = own_held[h].astype(F32) + other_held[h].astype(F32)
+        dq_held[:, cols] = total.astype(BF16)
+    stores[4].start()
+    loads[2].wait()
     for h in range(HEADS):
         cols = slice(h * DIM, (h + 1) * DIM)
         gk_held[:, cols] = gp_held[h, 0:2, :].astype(BF16)
         gv_held[:, cols] = gp_held[h, 2:4, :].astype(BF16)
-    for store in stores[-2:]:
-        store.start()
+    stores[5].start()
+    stores[6].start()
+    for n in range(4):
+        loads[3 + n].wait()
+        stores[n].start()
     for store in stores:
         store.wait()
 
@@ -430,13 +448,14 @@
     grads = pl.pallas_call(
         kernel,
         out_shape=(
-            jax.ShapeDtypeStruct((SLOTS, WIDTH), BF16),
+            jax.ShapeDtypeStruct((HEADS, SLOTS, DIM), BF16),
+            jax.ShapeDtypeStruct((HEADS, SLOTS, DIM), BF16),
             jax.ShapeDtypeStruct((ROWS, WIDTH), BF16),
             jax.ShapeDtypeStruct((ROWS, WIDTH), BF16),
             jax.ShapeDtypeStruct((16, 8, DIM), F32),
         ),
         in_specs=[hbm] * 8,
-        out_specs=(hbm,) * 4,
+        out_specs=(hbm,) * 5,
         scratch_shapes=[
             V((2, WIDTH), BF16),
             V((2, WIDTH), BF16),
@@ -480,12 +499,10 @@
             V((16, 8, DIM), F32),
             V((16, SLOTS, DIM), BF16),
             V((16, SLOTS, DIM), BF16),
-            V((16, SLOTS, DIM), F32),
-            V((SLOTS, WIDTH), BF16),
             V((ROWS, WIDTH), BF16),
             V((ROWS, WIDTH), BF16),
             pltpu.SemaphoreType.DMA((8,)),
-            pltpu.SemaphoreType.DMA((4,)),
+            pltpu.SemaphoreType.DMA((5,)),
             pltpu.SemaphoreType.DMA((KINDS,)),
             pltpu.SemaphoreType.DMA((KINDS,)),
             pltpu.SemaphoreType.DMA((2, 4)),
@@ -497,19 +514,18 @@
         prompt_k, prompt_v, rewards, mask_pos[0], comp_q[0, 0], comp_k[0, 0], comp_v[0, 0],
         grad_out[0, 0],
     )
-    wide = [jax.ShapeDtypeStruct(grad.shape, BF16) for grad in grads[:3]]
-    thin = [jax.ShapeDtypeStruct((2, WIDTH), BF16)] * 2
+    shapes = [(SLOTS, WIDTH), (ROWS, WIDTH), (ROWS, WIDTH), (2, WIDTH), (2, WIDTH)]
     dq, dk, dv, gk, gv = pl.pallas_call(
         store_all,
-        out_shape=wide + thin,
-        in_specs=[hbm] * 4,
+        out_shape=[jax.ShapeDtypeStruct(shape, BF16) for shape in shapes],
+        in_specs=[hbm] * 5,
         out_specs=[hbm] * 5,
-        scratch_shapes=[V(grad.shape, BF16) for grad in grads[:3]]
+        scratch_shapes=[V(grad.shape, grad.dtype) for grad in grads]
         + [
-            V((16, 8, DIM), F32),
+            V((SLOTS, WIDTH), BF16),
             V((2, WIDTH), BF16),
             V((2, WIDTH), BF16),
-            pltpu.SemaphoreType.DMA((6,)),
+            pltpu.SemaphoreType.DMA((7,)),
             pltpu.SemaphoreType.DMA((7,)),
         ],
         compiler_params=pltpu.CompilerParams(vmem_limit_bytes=60 * 1024 * 1024),

time: 45.3 us -> 44.2 us (0.976)
  Pallas kernels: 43.9 us -> 42.8 us
    pallas_call x2, Pallas kernels: 43.9 us -> 42.8 us  [the longest x1 40.5 us: shards(): pl.pallas_call(kernel, out_shape=(jax.ShapeDtypeStruct((HEADS, SLOTS, DIM...]
where the time goes in v11:
time: 44.2 us; the launch traced here: 44.1 us
  Pallas kernels  42.8 us (97%)
  between operations  1.29 us (3%)
    pallas_call x1, Pallas kernels, shards(): pl.pallas_call(kernel, out_shape=(jax.ShapeDtypeStruct((HEADS, SLOTS, DIM...  40.5 us
    pallas_call x1, Pallas kernels, shards(): pl.pallas_call(store_all, out_shape=[jax.ShapeDtypeStruct(shape, BF16) fo...  2.28 us

profile of v11, /device:TPU:1, one launch (start us, length us, event | category | flops | bytes accessed | tf_op | source)
XLA Modules:
  0.0 44.1 jit_solution(791078791922574036)
XLA Ops:
  1.3 40.5 %shard_map.119 = (bf16[16,64,128]{2,1,0:T(8,128)(2,1)}, bf16[16,64,128]{2,1,0:T(8,128)(2,1)}, bf16[128,2048]{1,0:T(8,128)(2,1)}, bf16[128,2048]{1,0:T(8,128)(2,1)}, f32[16,8,128]{2,1,0:T(8,128)}) custom-call(bf16[2,2048]{1,0:T(2,128)(2,1)} %pk_hbm.1, bf16[2,2048]{1,0:T(2,128)(2,1)} %pv_hbm.1, f32[1,1]{1,0:T(1,128)S(6)} %copy.13.rw_hbm, s32[1,64]{1,0:T(1,128)} %bitcast.12, ...), custom_call_target="tpu_custom_call" | custom-call | tf_op jit(solution)/shard_map/pallas_call | solution.py:448
  41.8 2.3 %shard_map.120 = (bf16[64,2048]{1,0:T(8,128)(2,1)}, bf16[128,2048]{1,0:T(8,128)(2,1)}, bf16[128,2048]{1,0:T(8,128)(2,1)}, bf16[2,2048]{1,0:T(2,128)(2,1)}, bf16[2,2048]{1,0:T(2,128)(2,1)}) custom-call(bf16[16,64,128]{2,1,0:T(8,128)(2,1)} %get-tuple-element.15.own, bf16[16,64,128]{2,1,0:T(8,128)(2,1)} %get-tuple-element.16.other, ...), custom_call_target="tpu_custom_call" | custom-call | tf_op jit(solution)/shard_map/pallas_call | solution.py:518

commit v12 on v11

--- a/solution.py
+++ b/solution.py
@@ -73,8 +73,8 @@
         flipped(z_lo, dz) * 8 + flipped(x_lo, dl) * 4 + flipped(x_hi, dh) * 2 + flipped(core, dc)
         for dz, dl, dh, dc in flips
     ]
-    z_others = [lax.rem(z_hi + k, 4) for k in range(1, 4)]
-    y_others = [lax.rem(y + k, 4) for k in range(1, 4)]
+    z_others = [lax.rem(z_hi + k, 4) for k in (2, 1, 3)]
+    y_others = [lax.rem(y + k, 4) for k in (2, 1, 3)]
 
     def remote(kind, src, dst, device):
         return pltpu.make_async_remote_copy(
@@ -103,16 +103,18 @@
             )
         )
     ]
-    for load in loads:
+    for load in loads[:4]:
         load.start()
 
     barrier = pltpu.get_barrier_semaphore()
-    for b in a_others:
-        pl.semaphore_signal(barrier, inc=1, device_id=a_peer(b), device_id_type=MESH)
     for b in z_others:
         pl.semaphore_signal(barrier, inc=1, device_id=z_peer(b), device_id_type=MESH)
     for b in y_others:
         pl.semaphore_signal(barrier, inc=1, device_id=y_peer(b), device_id_type=MESH)
+    for b in a_others:
+        pl.semaphore_signal(barrier, inc=1, device_id=a_peer(b), device_id_type=MESH)
+    for load in loads[4:]:
+        load.start()
 
     for load in loads[:4]:
         load.wait()
@@ -255,8 +257,7 @@
             prods[b, :, cols] = d
             part[b, 2:3, cols] = jnp.sum(exps[b, :, cols] * d, axis=0, keepdims=True)
 
-    near_first = [y_others[0], y_others[2], y_others[1]]
-    far_first = [y_others[1], y_others[0], y_others[2]]
+    near_first = y_others[1:] + y_others[:1]
     arrived(QUERY, xqr.at[pl.ds(0, 15)])
     key_block(y)
     for b in near_first:
@@ -287,7 +288,7 @@
     arrived(GRAD, xgr.at[pl.ds(0, 15)])
     q_all = xqr[...].reshape(16 * SLOTS, DIM)
     g_all = xgr[...].reshape(16 * SLOTS, DIM)
-    for b in far_first:
+    for b in y_others:
         probabilities(b)
         sbv[b] = dot_nn(pw[b], g_all).astype(BF16)
         remote(YSUM_V, sbv.at[b], rv.at[y], y_peer(b)).start()
@@ -307,7 +308,7 @@
             dscore = exps[b, :, cols] * (prods[b, :, cols] - inner[:, cols])
             ds[b, :, cols] = (dscore * weights[:, cols]).astype(BF16)
 
-    for b in far_first:
+    for b in y_others:
         finish(b)
         sbk[b] = dot_nn(ds[b], q_all).astype(BF16)
         remote(YSUM_K, sbk.at[b], rk.at[y], y_peer(b)).start()

time: 44.2 us -> 44 us (level)
  no operation moved by 1% of the time
where the time goes in v12:
time: 44 us; the launch traced here: 43.8 us
  Pallas kernels  42.5 us (97%)
  between operations  1.29 us (3%)
    pallas_call x1, Pallas kernels, shards(): pl.pallas_call(kernel, out_shape=(jax.ShapeDtypeStruct((HEADS, SLOTS, DIM...  40.2 us
    pallas_call x1, Pallas kernels, shards(): pl.pallas_call(store_all, out_shape=[jax.ShapeDtypeStruct(shape, BF16) fo...  2.28 us

profile of v12, /device:TPU:1, one launch (start us, length us, event | category | flops | bytes accessed | tf_op | source)
XLA Modules:
  0.0 43.8 jit_solution(16194566308209052739)
XLA Ops:
  1.3 40.2 %shard_map.119 = (bf16[16,64,128]{2,1,0:T(8,128)(2,1)}, bf16[16,64,128]{2,1,0:T(8,128)(2,1)}, bf16[128,2048]{1,0:T(8,128)(2,1)}, bf16[128,2048]{1,0:T(8,128)(2,1)}, f32[16,8,128]{2,1,0:T(8,128)}) custom-call(bf16[2,2048]{1,0:T(2,128)(2,1)} %pk_hbm.1, bf16[2,2048]{1,0:T(2,128)(2,1)} %pv_hbm.1, f32[1,1]{1,0:T(1,128)S(6)} %copy.13.rw_hbm, s32[1,64]{1,0:T(1,128)} %bitcast.12, ...), custom_call_target="tpu_custom_call" | custom-call | tf_op jit(solution)/shard_map/pallas_call | solution.py:449
  41.5 2.3 %shard_map.120 = (bf16[64,2048]{1,0:T(8,128)(2,1)}, bf16[128,2048]{1,0:T(8,128)(2,1)}, bf16[128,2048]{1,0:T(8,128)(2,1)}, bf16[2,2048]{1,0:T(2,128)(2,1)}, bf16[2,2048]{1,0:T(2,128)(2,1)}) custom-call(bf16[16,64,128]{2,1,0:T(8,128)(2,1)} %get-tuple-element.15.own, bf16[16,64,128]{2,1,0:T(8,128)(2,1)} %get-tuple-element.16.other, ...), custom_call_target="tpu_custom_call" | custom-call | tf_op jit(solution)/shard_map/pallas_call | solution.py:519

commit v13 on v12

--- a/solution.py
+++ b/solution.py
@@ -148,6 +148,9 @@
     picked = dot_tn(pick, cq[...])[:SLOTS].astype(BF16)
     for h in range(HEADS):
         xq[h] = picked[:, h * DIM : (h + 1) * DIM]
+    for b in a_others[:4]:
+        remote(QUERY, xq.at[b], xqr.at[a], a_peer(b)).start()
+    xqr[a] = xq[a]
     loads[5].wait()
     for h in range(HEADS):
         xg[h] = go[:, h * DIM : (h + 1) * DIM]
@@ -210,9 +213,8 @@
     gsum[...] = jnp.concatenate([count16, reward16, jnp.zeros((6, DIM), F32)], axis=0)
     for b in z_others:
         remote(ZSUM, gsum, gsumr.at[z_hi], z_peer(b)).start()
-    for b in a_others:
+    for b in a_others[4:]:
         remote(QUERY, xq.at[b], xqr.at[a], a_peer(b)).start()
-    xqr[a] = xq[a]
     for b in a_others:
         remote(GRAD, xg.at[b], xgr.at[a], a_peer(b)).start()
     xgr[a] = xg[a]
@@ -285,15 +287,14 @@
             exps[b, :, cols] = p
             pw[b, :, cols] = (p * weights[:, cols]).astype(BF16)
 
+    for b in y_others + [y]:
+        probabilities(b)
     arrived(GRAD, xgr.at[pl.ds(0, 15)])
     q_all = xqr[...].reshape(16 * SLOTS, DIM)
     g_all = xgr[...].reshape(16 * SLOTS, DIM)
     for b in y_others:
-        probabilities(b)
         sbv[b] = dot_nn(pw[b], g_all).astype(BF16)
         remote(YSUM_V, sbv.at[b], rv.at[y], y_peer(b)).start()
-    probabilities(y)
-
     value_block(y)
     for b in near_first:
         along_y(1, vb, b, b).wait_recv()
@@ -328,11 +329,6 @@
         grad_q = dot_tn(ds[:, :, t * 128 : (t + 1) * 128].reshape(PROMPT, 2 * SLOTS), keys)
         dqs[2 * t] = grad_q[:SLOTS].astype(BF16)
         dqs[2 * t + 1] = grad_q[SLOTS:].astype(BF16)
-    for b in a_others:
-        remote(DQ, dqs.at[b], dqr.at[a], a_peer(b)).start()
-    own_part = pltpu.make_async_copy(dqs.at[a], dqr.at[a], out_sem.at[4])
-    own_part.start()
-
     def next_sum(total, kind_y, received, held, send, kind_z, target):
         arrived(kind_y, received.at[pl.ds(0, 3)])
         for b in y_others:
@@ -343,6 +339,10 @@
             remote(kind_z, send.at[b], target.at[z_hi], z_peer(b)).start()
 
     next_sum(grad_v, YSUM_V, rv, hv, szv, ZSUM_V, rzv)
+    for b in a_others:
+        remote(DQ, dqs.at[b], dqr.at[a], a_peer(b)).start()
+    own_part = pltpu.make_async_copy(dqs.at[a], dqr.at[a], out_sem.at[4])
+    own_part.start()
     next_sum(grad_k, YSUM_K, rk, hk, szk, ZSUM_K, rzk)
 
     arrived(FIN, fr.at[pl.ds(0, 15)])
@@ -429,6 +429,9 @@
         total = own_held[h].astype(F32) + other_held[h].astype(F32)
         dq_held[:, cols] = total.astype(BF16)
     stores[4].start()
+    for n in range(4):
+        loads[3 + n].wait()
+        stores[n].start()
     loads[2].wait()
     for h in range(HEADS):
         cols = slice(h * DIM, (h + 1) * DIM)
@@ -436,9 +439,6 @@
         gv_held[:, cols] = gp_held[h, 2:4, :].astype(BF16)
     stores[5].start()
     stores[6].start()
-    for n in range(4):
-        loads[3 + n].wait()
-        stores[n].start()
     for store in stores:
         store.wait()
 

time: 44 us -> 44.7 us (1.016)
  Pallas kernels: 42.5 us -> 43.3 us
    pallas_call x1, Pallas kernels: 40.2 us -> 41 us  [shards(): pl.pallas_call(kernel, out_shape=(jax.ShapeDtypeStruct((HEADS, SLOTS, DIM...]
where the time goes in v13:
time: 44.7 us; the launch traced here: 44.6 us
  Pallas kernels  43.3 us (97%)
  between operations  1.29 us (3%)
    pallas_call x1, Pallas kernels, shards(): pl.pallas_call(kernel, out_shape=(jax.ShapeDtypeStruct((HEADS, SLOTS, DIM...  41 us
    pallas_call x1, Pallas kernels, shards(): pl.pallas_call(store_all, out_shape=[jax.ShapeDtypeStruct(shape, BF16) fo...  2.28 us

profile of v13, /device:TPU:1, one launch (start us, length us, event | category | flops | bytes accessed | tf_op | source)
XLA Modules:
  0.0 44.6 jit_solution(4781155251030157980)
XLA Ops:
  1.3 41.0 %shard_map.119 = (bf16[16,64,128]{2,1,0:T(8,128)(2,1)}, bf16[16,64,128]{2,1,0:T(8,128)(2,1)}, bf16[128,2048]{1,0:T(8,128)(2,1)}, bf16[128,2048]{1,0:T(8,128)(2,1)}, f32[16,8,128]{2,1,0:T(8,128)}) custom-call(bf16[2,2048]{1,0:T(2,128)(2,1)} %pk_hbm.1, bf16[2,2048]{1,0:T(2,128)(2,1)} %pv_hbm.1, f32[1,1]{1,0:T(1,128)S(6)} %copy.13.rw_hbm, s32[1,64]{1,0:T(1,128)} %bitcast.12, ...), custom_call_target="tpu_custom_call" | custom-call | tf_op jit(solution)/shard_map/pallas_call | solution.py:449
  42.3 2.3 %shard_map.120 = (bf16[64,2048]{1,0:T(8,128)(2,1)}, bf16[128,2048]{1,0:T(8,128)(2,1)}, bf16[128,2048]{1,0:T(8,128)(2,1)}, bf16[2,2048]{1,0:T(2,128)(2,1)}, bf16[2,2048]{1,0:T(2,128)(2,1)}) custom-call(bf16[16,64,128]{2,1,0:T(8,128)(2,1)} %get-tuple-element.15.own, bf16[16,64,128]{2,1,0:T(8,128)(2,1)} %get-tuple-element.16.other, ...), custom_call_target="tpu_custom_call" | custom-call | tf_op jit(solution)/shard_map/pallas_call | solution.py:519

commit v14 on v12

--- a/solution.py
+++ b/solution.py
@@ -285,15 +285,14 @@
             exps[b, :, cols] = p
             pw[b, :, cols] = (p * weights[:, cols]).astype(BF16)
 
+    for b in y_others + [y]:
+        probabilities(b)
     arrived(GRAD, xgr.at[pl.ds(0, 15)])
     q_all = xqr[...].reshape(16 * SLOTS, DIM)
     g_all = xgr[...].reshape(16 * SLOTS, DIM)
     for b in y_others:
-        probabilities(b)
         sbv[b] = dot_nn(pw[b], g_all).astype(BF16)
         remote(YSUM_V, sbv.at[b], rv.at[y], y_peer(b)).start()
-    probabilities(y)
-
     value_block(y)
     for b in near_first:
         along_y(1, vb, b, b).wait_recv()
@@ -429,6 +428,9 @@
         total = own_held[h].astype(F32) + other_held[h].astype(F32)
         dq_held[:, cols] = total.astype(BF16)
     stores[4].start()
+    for n in range(4):
+        loads[3 + n].wait()
+        stores[n].start()
     loads[2].wait()
     for h in range(HEADS):
         cols = slice(h * DIM, (h + 1) * DIM)
@@ -436,9 +438,6 @@
         gv_held[:, cols] = gp_held[h, 2:4, :].astype(BF16)
     stores[5].start()
     stores[6].start()
-    for n in range(4):
-        loads[3 + n].wait()
-        stores[n].start()
     for store in stores:
         store.wait()
 

time: 44 us -> 44.2 us (level)
  no operation moved by 1% of the time
where the time goes in v14:
time: 44.2 us; the launch traced here: 44 us
  Pallas kernels  42.7 us (97%)
  between operations  1.29 us (3%)
    pallas_call x1, Pallas kernels, shards(): pl.pallas_call(kernel, out_shape=(jax.ShapeDtypeStruct((HEADS, SLOTS, DIM...  40.5 us
    pallas_call x1, Pallas kernels, shards(): pl.pallas_call(store_all, out_shape=[jax.ShapeDtypeStruct(shape, BF16) fo...  2.28 us

profile of v14, /device:TPU:1, one launch (start us, length us, event | category | flops | bytes accessed | tf_op | source)
XLA Modules:
  0.0 44.0 jit_solution(10048695370986413750)
XLA Ops:
  1.3 40.5 %shard_map.119 = (bf16[16,64,128]{2,1,0:T(8,128)(2,1)}, bf16[16,64,128]{2,1,0:T(8,128)(2,1)}, bf16[128,2048]{1,0:T(8,128)(2,1)}, bf16[128,2048]{1,0:T(8,128)(2,1)}, f32[16,8,128]{2,1,0:T(8,128)}) custom-call(bf16[2,2048]{1,0:T(2,128)(2,1)} %pk_hbm.1, bf16[2,2048]{1,0:T(2,128)(2,1)} %pv_hbm.1, f32[1,1]{1,0:T(1,128)S(6)} %copy.13.rw_hbm, s32[1,64]{1,0:T(1,128)} %bitcast.12, ...), custom_call_target="tpu_custom_call" | custom-call | tf_op jit(solution)/shard_map/pallas_call | solution.py:448
  41.8 2.3 %shard_map.120 = (bf16[64,2048]{1,0:T(8,128)(2,1)}, bf16[128,2048]{1,0:T(8,128)(2,1)}, bf16[128,2048]{1,0:T(8,128)(2,1)}, bf16[2,2048]{1,0:T(2,128)(2,1)}, bf16[2,2048]{1,0:T(2,128)(2,1)}) custom-call(bf16[16,64,128]{2,1,0:T(8,128)(2,1)} %get-tuple-element.15.own, bf16[16,64,128]{2,1,0:T(8,128)(2,1)} %get-tuple-element.16.other, ...), custom_call_target="tpu_custom_call" | custom-call | tf_op jit(solution)/shard_map/pallas_call | solution.py:518

commit v15 on v14

--- a/solution.py
+++ b/solution.py
@@ -249,13 +249,14 @@
             part[b, 0:1, cols] = m
             part[b, 1:2, cols] = jnp.sum(e, axis=0, keepdims=True)
 
-    def value_block(b):
-        block = vb[b].reshape(128, DIM)
+    def value_blocks(b):
+        block = vb[b : b + 2].reshape(256, DIM)
         for n in range(4):
             cols = slice(n * 256, (n + 1) * 256)
             d = dot_nt(block, xgr[4 * n : 4 * n + 4].reshape(256, DIM)) * SCALE
-            prods[b, :, cols] = d
-            part[b, 2:3, cols] = jnp.sum(exps[b, :, cols] * d, axis=0, keepdims=True)
+            prods[b : b + 2, :, cols] = d.reshape(2, 128, 256)
+            p = exps[b : b + 2, :, cols].reshape(256, 256)
+            part[b, 2:3, cols] = jnp.sum(p * d, axis=0, keepdims=True)
 
     near_first = y_others[1:] + y_others[:1]
     arrived(QUERY, xqr.at[pl.ds(0, 15)])
@@ -293,12 +294,12 @@
     for b in y_others:
         sbv[b] = dot_nn(pw[b], g_all).astype(BF16)
         remote(YSUM_V, sbv.at[b], rv.at[y], y_peer(b)).start()
-    value_block(y)
     for b in near_first:
         along_y(1, vb, b, b).wait_recv()
-        value_block(b)
+    value_blocks(0)
+    value_blocks(2)
     inner = stats[2:3] * (fo * inv * SCALE)
-    for b in range(4):
+    for b in (0, 2):
         inner = inner + part[b, 2:3, :]
 
     def finish(b):

time: 44.2 us -> 43.8 us (level)
  no operation moved by 1% of the time
where the time goes in v15:
time: 43.8 us; the launch traced here: 43.7 us
  Pallas kernels  42.4 us (97%)
  between operations  1.29 us (3%)
    pallas_call x1, Pallas kernels, shards(): pl.pallas_call(kernel, out_shape=(jax.ShapeDtypeStruct((HEADS, SLOTS, DIM...  40.1 us
    pallas_call x1, Pallas kernels, shards(): pl.pallas_call(store_all, out_shape=[jax.ShapeDtypeStruct(shape, BF16) fo...  2.28 us

profile of v15, /device:TPU:1, one launch (start us, length us, event | category | flops | bytes accessed | tf_op | source)
XLA Modules:
  0.0 43.7 jit_solution(3479544805586492583)
XLA Ops:
  1.3 40.1 %shard_map.119 = (bf16[16,64,128]{2,1,0:T(8,128)(2,1)}, bf16[16,64,128]{2,1,0:T(8,128)(2,1)}, bf16[128,2048]{1,0:T(8,128)(2,1)}, bf16[128,2048]{1,0:T(8,128)(2,1)}, f32[16,8,128]{2,1,0:T(8,128)}) custom-call(bf16[2,2048]{1,0:T(2,128)(2,1)} %pk_hbm.1, bf16[2,2048]{1,0:T(2,128)(2,1)} %pv_hbm.1, f32[1,1]{1,0:T(1,128)S(6)} %copy.13.rw_hbm, s32[1,64]{1,0:T(1,128)} %bitcast.12, ...), custom_call_target="tpu_custom_call" | custom-call | tf_op jit(solution)/shard_map/pallas_call | solution.py:449
  41.4 2.3 %shard_map.120 = (bf16[64,2048]{1,0:T(8,128)(2,1)}, bf16[128,2048]{1,0:T(8,128)(2,1)}, bf16[128,2048]{1,0:T(8,128)(2,1)}, bf16[2,2048]{1,0:T(2,128)(2,1)}, bf16[2,2048]{1,0:T(2,128)(2,1)}) custom-call(bf16[16,64,128]{2,1,0:T(8,128)(2,1)} %get-tuple-element.15.own, bf16[16,64,128]{2,1,0:T(8,128)(2,1)} %get-tuple-element.16.other, ...), custom_call_target="tpu_custom_call" | custom-call | tf_op jit(solution)/shard_map/pallas_call | solution.py:519

commit v16 on v15

--- a/solution.py
+++ b/solution.py
@@ -250,12 +250,12 @@
             part[b, 1:2, cols] = jnp.sum(e, axis=0, keepdims=True)
 
     def value_blocks(b):
-        block = vb[b : b + 2].reshape(256, DIM)
+        block = vb[...].reshape(PROMPT, DIM)
         for n in range(4):
             cols = slice(n * 256, (n + 1) * 256)
             d = dot_nt(block, xgr[4 * n : 4 * n + 4].reshape(256, DIM)) * SCALE
-            prods[b : b + 2, :, cols] = d.reshape(2, 128, 256)
-            p = exps[b : b + 2, :, cols].reshape(256, 256)
+            prods[:, :, cols] = d.reshape(4, 128, 256)
+            p = exps[:, :, cols].reshape(PROMPT, 256)
             part[b, 2:3, cols] = jnp.sum(p * d, axis=0, keepdims=True)
 
     near_first = y_others[1:] + y_others[:1]
@@ -297,9 +297,8 @@
     for b in near_first:
         along_y(1, vb, b, b).wait_recv()
     value_blocks(0)
-    value_blocks(2)
     inner = stats[2:3] * (fo * inv * SCALE)
-    for b in (0, 2):
+    for b in (0,):
         inner = inner + part[b, 2:3, :]
 
     def finish(b):

time: 43.8 us -> 43.8 us (level)
  no operation moved by 1% of the time
where the time goes in v16:
time: 43.8 us; the launch traced here: 43.7 us
  Pallas kernels  42.4 us (97%)
  between operations  1.29 us (3%)
    pallas_call x1, Pallas kernels, shards(): pl.pallas_call(kernel, out_shape=(jax.ShapeDtypeStruct((HEADS, SLOTS, DIM...  40.1 us
    pallas_call x1, Pallas kernels, shards(): pl.pallas_call(store_all, out_shape=[jax.ShapeDtypeStruct(shape, BF16) fo...  2.28 us

profile of v16, /device:TPU:1, one launch (start us, length us, event | category | flops | bytes accessed | tf_op | source)
XLA Modules:
  0.0 43.7 jit_solution(8561093775894437470)
XLA Ops:
  1.3 40.1 %shard_map.119 = (bf16[16,64,128]{2,1,0:T(8,128)(2,1)}, bf16[16,64,128]{2,1,0:T(8,128)(2,1)}, bf16[128,2048]{1,0:T(8,128)(2,1)}, bf16[128,2048]{1,0:T(8,128)(2,1)}, f32[16,8,128]{2,1,0:T(8,128)}) custom-call(bf16[2,2048]{1,0:T(2,128)(2,1)} %pk_hbm.1, bf16[2,2048]{1,0:T(2,128)(2,1)} %pv_hbm.1, f32[1,1]{1,0:T(1,128)S(6)} %copy.13.rw_hbm, s32[1,64]{1,0:T(1,128)} %bitcast.12, ...), custom_call_target="tpu_custom_call" | custom-call | tf_op jit(solution)/shard_map/pallas_call | solution.py:448
  41.4 2.3 %shard_map.120 = (bf16[64,2048]{1,0:T(8,128)(2,1)}, bf16[128,2048]{1,0:T(8,128)(2,1)}, bf16[128,2048]{1,0:T(8,128)(2,1)}, bf16[2,2048]{1,0:T(2,128)(2,1)}, bf16[2,2048]{1,0:T(2,128)(2,1)}) custom-call(bf16[16,64,128]{2,1,0:T(8,128)(2,1)} %get-tuple-element.15.own, bf16[16,64,128]{2,1,0:T(8,128)(2,1)} %get-tuple-element.16.other, ...), custom_call_target="tpu_custom_call" | custom-call | tf_op jit(solution)/shard_map/pallas_call | solution.py:518

commit v17 on v15

--- a/solution.py
+++ b/solution.py
@@ -321,9 +321,6 @@
     keys = kb[...].reshape(PROMPT, DIM)
     grad_v = dot_nn(pw[y], g_all)
     grad_k = dot_nn(ds[y], q_all)
-    for b in a_others:
-        remote(FIN, fs.at[lax.div(b, 2)], fr.at[a], a_peer(b)).start()
-    fr[a] = fs[lax.div(a, 2)]
     for t in range(8):
         grad_q = dot_tn(ds[:, :, t * 128 : (t + 1) * 128].reshape(PROMPT, 2 * SLOTS), keys)
         dqs[2 * t] = grad_q[:SLOTS].astype(BF16)
@@ -332,6 +329,9 @@
         remote(DQ, dqs.at[b], dqr.at[a], a_peer(b)).start()
     own_part = pltpu.make_async_copy(dqs.at[a], dqr.at[a], out_sem.at[4])
     own_part.start()
+    for b in a_others:
+        remote(FIN, fs.at[lax.div(b, 2)], fr.at[a], a_peer(b)).start()
+    fr[a] = fs[lax.div(a, 2)]
 
     def next_sum(total, kind_y, received, held, send, kind_z, target):
         arrived(kind_y, received.at[pl.ds(0, 3)])

time: 43.8 us -> 43.8 us (level)
  no operation moved by 1% of the time
where the time goes in v17:
time: 43.8 us; the launch traced here: 43.7 us
  Pallas kernels  42.4 us (97%)
  between operations  1.29 us (3%)
    pallas_call x1, Pallas kernels, shards(): pl.pallas_call(kernel, out_shape=(jax.ShapeDtypeStruct((HEADS, SLOTS, DIM...  40.1 us
    pallas_call x1, Pallas kernels, shards(): pl.pallas_call(store_all, out_shape=[jax.ShapeDtypeStruct(shape, BF16) fo...  2.28 us

profile of v17, /device:TPU:1, one launch (start us, length us, event | category | flops | bytes accessed | tf_op | source)
XLA Modules:
  0.0 43.7 jit_solution(10260530347231310801)
XLA Ops:
  1.3 40.1 %shard_map.119 = (bf16[16,64,128]{2,1,0:T(8,128)(2,1)}, bf16[16,64,128]{2,1,0:T(8,128)(2,1)}, bf16[128,2048]{1,0:T(8,128)(2,1)}, bf16[128,2048]{1,0:T(8,128)(2,1)}, f32[16,8,128]{2,1,0:T(8,128)}) custom-call(bf16[2,2048]{1,0:T(2,128)(2,1)} %pk_hbm.1, bf16[2,2048]{1,0:T(2,128)(2,1)} %pv_hbm.1, f32[1,1]{1,0:T(1,128)S(6)} %copy.13.rw_hbm, s32[1,64]{1,0:T(1,128)} %bitcast.12, ...), custom_call_target="tpu_custom_call" | custom-call | tf_op jit(solution)/shard_map/pallas_call | solution.py:449
  41.4 2.3 %shard_map.120 = (bf16[64,2048]{1,0:T(8,128)(2,1)}, bf16[128,2048]{1,0:T(8,128)(2,1)}, bf16[128,2048]{1,0:T(8,128)(2,1)}, bf16[2,2048]{1,0:T(2,128)(2,1)}, bf16[2,2048]{1,0:T(2,128)(2,1)}) custom-call(bf16[16,64,128]{2,1,0:T(8,128)(2,1)} %get-tuple-element.15.own, bf16[16,64,128]{2,1,0:T(8,128)(2,1)} %get-tuple-element.16.other, ...), custom_call_target="tpu_custom_call" | custom-call | tf_op jit(solution)/shard_map/pallas_call | solution.py:519
